TPU v7x, 32 devices: a whole 2x2x4 slice. The times are simulated.
32 devices in a mesh: gx: 8 (over z, x), gy: 4 (over y, core).
Axes of the slice: x: 2, y: 2, z: 4, core: 2. Of those that a mesh axis runs over, the one named last changes fastest.
Arguments:
- body_force: float32 [3, 128, 128, 128], P(None, 'gx', 'gy'), may hold values from -30 to 30, as said below
- fixed_dofs: int32 [3, 128, 128, 128], P(None, 'gx', 'gy'), may hold values 0 or 1
- load_nodes: int32 [512, 3], replicated, may hold values from 0 to 127, as said below
- load_forces: float32 [3, 512], replicated, may hold values from -32 to 32
- frequencies: float32 [3, 64], replicated, may hold values from -24 to 24
- hidden_weights: float32 [3, 128, 128], replicated, may hold values from -0.5 to 0.5
- hidden_biases: float32 [3, 128], replicated, may hold values from -6 to 6
- output_weights: float32 [128], replicated, may hold values from -3 to 3
- output_bias: float32 [1], replicated, may hold values from -3 to 3
Outputs:
- displacement: float32 [3, 128, 128, 128], P(None, 'gx', 'gy')
- density: float32 [128, 128, 128], P('gx', 'gy')
Inputs may be any that keep to these rules, and one draw needn't show every extreme that they name: `load_nodes`: row p gives the x, y and z index of point load p's node: column 0 below 128, column 1 below 128, column 2 below 128; several loads may share a node. `body_force`: finite values of order one to ten.
All inputs are finite; a program needn't handle non-finite values. No bound on the sum of `fixed_dofs` on one device may be relied on, other than what follows from the above.
Results may differ from a plain program's by a relative error of at most 0.00013.
Values sent between devices are 32-bit elements; how exact they have to be, the bound alone decides.
A program may use at most 128 MiB of HBM per device.

v0:
```python
import math

import jax
import jax.numpy as jnp
import numpy as np
from jax import lax
from jax.sharding import PartitionSpec as P

CF = 4
ITERS = 2


full_turn = 2.0 * math.pi
highest = lax.Precision.HIGHEST


def extended(array, sides, width):
    for axis, dim in sides:
        count, length = (lax.axis_size(axis), array.shape[dim])
        up = [(i, (i + 1) % count) for i in range(count - 1)]
        down = [(j, i) for i, j in up]
        last = lax.slice_in_dim(array, length - width, length, axis=dim)
        leading = lax.slice_in_dim(array, 0, width, axis=dim)
        before = lax.ppermute(last, axis, up)
        after = lax.ppermute(leading, axis, down)
        array = jnp.concatenate([before, array, after], axis=dim)
    return array


def shifted(value, axis, steps):
    count = lax.axis_size(axis)
    leading, last = (max(0, -steps), min(count, count - steps))
    return lax.ppermute(value, axis, [(source, source + steps) for source in range(leading, last)])


def element_stiffness():
    poisson = 0.3
    lame_first = poisson / ((1.0 + poisson) * (1.0 - 2.0 * poisson))
    lame_second = 1.0 / (2.0 * (1.0 + poisson))
    elastic = np.zeros((6, 6))
    elastic[:3, :3] = lame_first
    elastic[np.arange(3), np.arange(3)] += 2.0 * lame_second
    elastic[np.arange(3, 6), np.arange(3, 6)] = lame_second
    gauss = 1.0 / math.sqrt(3.0)
    stiffness = np.zeros((24, 24))
    for point in range(8):
        where_at = [gauss * (2 * (point >> which & 1) - 1) for which in range(3)]
        strain = np.zeros((6, 24))
        for corner in range(8):
            signs = [2 * (corner >> which & 1) - 1 for which in range(3)]
            slopes = []
            for which in range(3):
                value = 0.25 * signs[which]
                for other in range(3):
                    if other != which:
                        value = value * (1.0 + signs[other] * where_at[other])
                slopes.append(value)
            column = 3 * corner
            strain[0, column] = slopes[0]
            strain[1, column + 1] = slopes[1]
            strain[2, column + 2] = slopes[2]
            strain[3, column] = slopes[1]
            strain[3, column + 1] = slopes[0]
            strain[4, column + 1] = slopes[2]
            strain[4, column + 2] = slopes[1]
            strain[5, column] = slopes[2]
            strain[5, column + 2] = slopes[0]
        stiffness = stiffness + strain.T @ elastic @ strain * 0.125
    return jnp.asarray(stiffness, dtype=jnp.float32)


def corner_offsets(corner):
    return (corner & 1, corner >> 1 & 1, corner >> 2 & 1)


def z_shift(values, offset):
    widths = [(0, 0)] * (values.ndim - 1)
    if offset > 0:
        return jnp.pad(values[..., 1:], widths + [(0, 1)])
    return jnp.pad(values[..., :-1], widths + [(1, 0)])


def coarse_density(
    begin_x,
    begin_y,
    count_x,
    count_y,
    count_z,
    total_x,
    total_y,
    total_z,
    frequencies,
    hidden_weights,
    hidden_biases,
    output_weights,
    output_bias,
):
    along_x = ((begin_x + jnp.arange(count_x, dtype=jnp.int32)).astype(jnp.float32) + 0.5) / float(
        total_x
    )
    along_y = ((begin_y + jnp.arange(count_y, dtype=jnp.int32)).astype(jnp.float32) + 0.5) / float(
        total_y
    )
    along_z = (jnp.arange(count_z, dtype=jnp.int32).astype(jnp.float32) + 0.5) / float(total_z)
    grid_shape = (count_x, count_y, count_z)
    centres = jnp.stack(
        [
            jnp.broadcast_to(along_x[:, None, None], grid_shape).reshape(-1),
            jnp.broadcast_to(along_y[None, :, None], grid_shape).reshape(-1),
            jnp.broadcast_to(along_z[None, None, :], grid_shape).reshape(-1),
        ],
        axis=0,
    )
    phases = (
        jnp.dot(frequencies.T, centres, precision=highest, preferred_element_type=jnp.float32)
        * full_turn
    )
    hidden = jnp.concatenate([jnp.sin(phases), jnp.cos(phases)], axis=0)
    for layer in range(hidden_weights.shape[0]):
        mixed = jnp.dot(
            hidden_weights[layer].T, hidden, precision=highest, preferred_element_type=jnp.float32
        )
        hidden = jax.nn.silu(mixed + hidden_biases[layer][:, None])
    logits = (
        jnp.dot(output_weights, hidden, precision=highest, preferred_element_type=jnp.float32)
        + output_bias[0]
    )
    return jax.nn.sigmoid(logits).reshape(grid_shape)


def upsample(coarse):
    across, along, height = coarse.shape
    spread = jnp.broadcast_to(
        coarse[:, None, :, None, :, None], (across, CF, along, CF, height, CF)
    )
    return spread.reshape(across * CF, along * CF, height * CF)


def inside_mask(begin_x, begin_y, count_x, count_y, height, total_x, total_y):
    index_x = begin_x + jnp.arange(count_x, dtype=jnp.int32)
    index_y = begin_y + jnp.arange(count_y, dtype=jnp.int32)
    valid_x = (index_x >= 0) & (index_x < total_x)
    valid_y = (index_y >= 0) & (index_y < total_y)
    inside = (valid_x[:, None, None] & valid_y[None, :, None]).astype(jnp.float32)
    return jnp.broadcast_to(inside, (count_x, count_y, height))


def cone_filter(padded, count_x, count_y):
    result = jnp.zeros((count_x, count_y, padded.shape[2]), jnp.float32)
    for shift_x in (-1, 0, 1):
        for shift_y in (-1, 0, 1):
            for shift_z in (-1, 0, 1):
                weight = 2.0 - math.sqrt(shift_x * shift_x + shift_y * shift_y + shift_z * shift_z)
                piece = padded[
                    1 + shift_x : 1 + shift_x + count_x, 1 + shift_y : 1 + shift_y + count_y
                ]
                if shift_z != 0:
                    piece = z_shift(piece, shift_z)
                result = result + weight * piece
    return result


def corner_products(nodes, young, stiffness):
    across, along, height = young.shape
    pieces = []
    for corner in range(8):
        off_x, off_y, off_z = corner_offsets(corner)
        piece = nodes[:, off_x : off_x + across, off_y : off_y + along]
        if off_z:
            piece = z_shift(piece, 1)
        pieces.append(piece)
    stacked = jnp.concatenate(pieces, axis=0).reshape(24, across * along * height)
    products = jnp.dot(stiffness, stacked, precision=highest, preferred_element_type=jnp.float32)
    return products.reshape(24, across, along, height) * young[None]


def all_forces(products):
    result = jnp.zeros(
        (3, products.shape[1] + 1, products.shape[2] + 1, products.shape[3]), jnp.float32
    )
    for corner in range(8):
        off_x, off_y, off_z = corner_offsets(corner)
        piece = jnp.pad(
            products[3 * corner : 3 * corner + 3],
            ((0, 0), (off_x, 1 - off_x), (off_y, 1 - off_y), (0, 0)),
        )
        if off_z:
            piece = z_shift(piece, -1)
        result = result + piece
    return result


def owned_forces(nodes, young, stiffness):
    planes, along, height = young.shape
    count = planes // CF

    def block(index):
        begin = index * CF
        nodes_block = lax.dynamic_slice_in_dim(nodes, begin, CF + 1, 1)
        young_block = lax.dynamic_slice_in_dim(young, begin, CF, 0)
        return all_forces(corner_products(nodes_block, young_block, stiffness))

    blocks = lax.map(block, jnp.arange(count, dtype=jnp.int32))
    main_part = jnp.moveaxis(blocks[:, :, :CF], 0, 1).reshape(3, planes, along + 1, height)
    spill = jnp.moveaxis(blocks[:, :, CF], 0, 1)
    main_part = jnp.pad(main_part, ((0, 0), (0, 1), (0, 0), (0, 0)))
    return main_part.at[:, CF::CF].add(spill)


def stiffness_diagonal(young_ext, stiffness):
    across, along = (young_ext.shape[0] - 1, young_ext.shape[1] - 1)
    entries = jnp.diagonal(stiffness)
    result = jnp.zeros((3, across, along, young_ext.shape[2]), jnp.float32)
    for corner in range(8):
        off_x, off_y, off_z = corner_offsets(corner)
        piece = young_ext[1 - off_x : 1 - off_x + across, 1 - off_y : 1 - off_y + along]
        if off_z:
            piece = z_shift(piece, -1)
        result = result + entries[3 * corner : 3 * corner + 3][:, None, None, None] * piece[None]
    return result


def per_device(
    body_force,
    fixed_dofs,
    load_nodes,
    load_forces,
    frequencies,
    hidden_weights,
    hidden_biases,
    output_weights,
    output_bias,
):
    stiffness = element_stiffness()
    cells_x, cells_y, height = (body_force.shape[1], body_force.shape[2], body_force.shape[3])
    total_x = cells_x * lax.axis_size("gx")
    total_y = cells_y * lax.axis_size("gy")
    block_x = lax.axis_index("gx")
    block_y = lax.axis_index("gy")
    start_x = block_x * cells_x
    start_y = block_y * cells_y
    network = (frequencies, hidden_weights, hidden_biases, output_weights, output_bias)
    inside_raw = inside_mask(
        start_x - 2, start_y - 2, cells_x + 4, cells_y + 4, height, total_x, total_y
    )
    own_coarse = coarse_density(
        block_x * (cells_x // CF),
        block_y * (cells_y // CF),
        cells_x // CF,
        cells_y // CF,
        height // CF,
        total_x // CF,
        total_y // CF,
        height // CF,
        *network
    )
    raw_padded = extended(upsample(own_coarse), (("gx", 0), ("gy", 1)), 2)
    filtered = cone_filter(raw_padded, cells_x + 1, cells_y + 1) / cone_filter(
        inside_raw, cells_x + 1, cells_y + 1
    )
    density = filtered[1:, 1:]
    inside_elements = inside_raw[1 : cells_x + 2, 1 : cells_y + 2]
    young_ext = (0.02 + 0.98 * filtered**3) * inside_elements
    free_dofs = 1.0 - fixed_dofs.astype(jnp.float32)
    jacobi = free_dofs * stiffness_diagonal(young_ext, stiffness) + (1.0 - free_dofs)
    local_x = load_nodes[:, 0] - start_x
    local_y = load_nodes[:, 1] - start_y
    mine = (local_x >= 0) & (local_x < cells_x) & (local_y >= 0) & (local_y < cells_y)
    index_x = jnp.where(mine, local_x, cells_x)
    index_y = jnp.where(mine, local_y, 0)
    loaded = body_force.at[:, index_x, index_y, load_nodes[:, 2]].add(load_forces, mode="drop")
    rhs = free_dofs * loaded
    displacement = jnp.zeros_like(rhs)
    residual = rhs
    scaled = residual / jacobi

    def scaled_norm(residual_now, scaled_now):
        return lax.psum(jnp.sum(residual_now * scaled_now), ("gx", "gy"))

    direction = scaled
    norm_now = scaled_norm(residual, scaled)
    for iteration in range(ITERS):
        upper = shifted(direction[:, :1], "gx", -1)
        taller = jnp.concatenate([direction, upper], axis=1)
        beside = shifted(taller[:, :, :1], "gy", -1)
        nodes = jnp.concatenate([taller, beside], axis=2)
        spread = owned_forces(nodes, young_ext[1:, 1:], stiffness)
        back_row = shifted(spread[:, :, cells_y:], "gy", 1)
        spread = jnp.concatenate([spread[:, :, :1] + back_row, spread[:, :, 1:cells_y]], axis=2)
        back_plane = shifted(spread[:, cells_x:], "gx", 1)
        forces = jnp.concatenate([spread[:, :1] + back_plane, spread[:, 1:cells_x]], axis=1)
        image = free_dofs * forces
        alpha = norm_now / lax.psum(jnp.sum(direction * image), ("gx", "gy"))
        displacement = displacement + alpha * direction
        residual = residual - alpha * image
        if iteration + 1 < ITERS:
            scaled = residual / jacobi
            norm_next = scaled_norm(residual, scaled)
            direction = scaled + norm_next / norm_now * direction
            norm_now = norm_next
    return (displacement, density)


def solution(mesh):
    return jax.shard_map(
        per_device,
        mesh=mesh,
        in_specs=(
            P(None, "gx", "gy", None),
            P(None, "gx", "gy", None),
            P(),
            P(),
            P(),
            P(),
            P(),
            P(),
            P(),
        ),
        out_specs=(P(None, "gx", "gy", None), P("gx", "gy", None)),
        check_vma=False,
    )
```

profile of v0, /device:TPU:0, one launch (start us, length us, event | category | flops | bytes accessed | tf_op | source)
XLA Modules:
  0.0 380.9 jit_solution(17953764170746472192)
XLA Ops:
  2.6 3.1 sine_bitcast_fusion
  5.6 1.8 fusion.14
  9.5 4.4 %broadcast_in_dim.97 = f32[4,4,8,4,32,4]{5,4,3,2,1,0:T(8,128)} broadcast(f32[4,8,32]{2,1,0:T(8,128)S(1)} %broadcast_in_dim.96), dimensions={0,2,4} | broadcast | bytes 266240 | tf_op jit(solution)/shard_map/broadcast_in_dim | solution.py:133
  13.9 8.2 %reshape.141 = f32[16,32,128]{2,1,0:T(8,128)S(1)} reshape(f32[4,4,8,4,32,4]{5,4,3,2,1,0:T(8,128)} %broadcast_in_dim.97) | data formatting | bytes 524288 | tf_op jit(solution)/shard_map/reshape | solution.py:136
  22.2 5.0 %collective-permute-start = (f32[2,32,128]{2,1,0:T(8,128)S(1)}, f32[2,32,128]{2,1,0:T(8,128)S(1)}, u32[]{:S(2)}, u32[]{:S(2)}) collective-permute-start(f32[2,32,128]{2,1,0:T(8,128)S(1)} %get-tuple-element.314), channel_id=1, source_target_pairs={{0,4},{4,8},{8,12},{12,16},{16,20},{20,24},{24,28},{1,5},{5,9},{9,... | collective-permute-start | bytes 98312 | tf_op jit(solution)/shard_map/ppermute | solution.py:24
  29.5 3.4 collective-permute-done.1
  34.3 16.5 %copy.77 = f32[3,16,32,128]{0,3,2,1:T(8,128)} copy(f32[3,16,32,128]{3,2,1,0:T(8,128)S(1)} %copy-done.13) | data formatting | bytes 1572864 | tf_op args[0]
  51.0 57.2 %scatter_fusion = f32[3,16,32,128]{0,3,2,1:T(8,128)} fusion(f32[3,16,32,128]{0,3,2,1:T(8,128)} %copy.77, s32[512]{0:T(512)S(1)} %bitcast.112, f32[512,3]{1,0:T(8,128)S(1)} %copy.78), kind=kCustom, calls=%fused_computation.1 | custom fusion | flops 1536 | bytes 24576 | tf_op jit(solution)/shard_map/scatter-add | solution.py:271
  108.2 19.5 %copy.79 = f32[3,16,32,128]{3,2,1,0:T(8,128)S(1)} copy(f32[3,16,32,128]{0,3,2,1:T(8,128)} %scatter_fusion) | data formatting | bytes 1572864 | tf_op jit(solution)/shard_map/scatter-add | solution.py:271
  132.6 4.2 %fusion.43 = (f32[17,33,128]{2,1,0:T(8,128)S(1)}, f32[17,33,128]{2,1,0:T(8,128)}) fusion(f32[17,33]{1,0:T(8,128)S(1)} %get-tuple-element.326, f32[17,33,127]{2,1,0:T(8,128)S(1)} %slice.691, f32[17,33]{1,0:T(8,128)S(1)} %get-tuple-element.321, f32[17,33,127]{2,1,0:T(8,128)S(1)} %slice.689, f32[17,33]{1,0:T(8,128)S(1)} %get-tuple-element.323, ...), kind=kLoop, calls=%fused_computation.151 | loop fusion | flops 7970688 | bytes 8090244 | tf_op jit(solution)/shard_map/mul | solution.py:263
  138.2 1.8 fusion.127
  141.3 4.7 %collective-permute-done.4 = f32[3,1,32,128]{3,2,1,0:T(8,128)S(1)} collective-permute-done((f32[3,1,32,128]{3,2,1,0:T(8,128)S(1)}, f32[3,1,32,128]{3,2,1,0:T(8,128)S(1)}, u32[]{:S(2)}, u32[]{:S(2)}) %collective-permute-start.4) | collective-permute-done | bytes 49184 | tf_op jit(solution)/shard_map/ppermute | solution.py:33
  147.3 3.8 collective-permute-done.5
  152.3 27.3 %while.26 = (s32[]{:T(128)}, f32[4,3,5,33,128]{4,3,2,1,0:T(8,128)}, s32[4]{0:T(128)S(1)}, f32[3,17,33,128]{3,2,1,0:T(8,128)S(1)}, f32[16,32,128]{2,1,0:T(8,128)}...) while((s32[]{:T(128)}, f32[4,3,5,33,128]{4,3,2,1,0:T(8,128)}, ...), condition=%wide.region_4.5_spmd.clone, body=%wide.region_3.4_spmd.sunk.clone.sunk | while | flops 114082952 | bytes 21380648 | solution.py:203
  154.2 2.2 fusion.152
  161.0 2.2 fusion.152
  167.9 2.2 fusion.152
  174.7 2.2 fusion.152
  182.9 4.6 %collective-permute-start.6 = (f32[3,17,1,128]{3,2,1,0:T(1,128)S(1)}, f32[3,17,1,128]{3,2,1,0:T(1,128)S(1)}, u32[]{:S(2)}, u32[]{:S(2)}) collective-permute-start(f32[3,17,1,128]{3,2,1,0:T(1,128)S(1)} %slice.902), channel_id=1, source_target_pairs={{0,1},{1,2},{2,3},{4,5},{5,6},{6,7},{8,9},{9,10},{10,11},{12,13},{... | collective-permute-start | bytes 78344 | tf_op jit(solution)/shard_map/ppermute | solution.py:33
  188.4 4.5 %collective-permute-start.7 = (f32[3,1,32,128]{3,2,1,0:T(8,128)S(1)}, f32[3,1,32,128]{3,2,1,0:T(8,128)S(1)}, u32[]{:S(2)}, u32[]{:S(2)}) collective-permute-start(f32[3,1,32,128]{3,2,1,0:T(8,128)S(1)} %pad_maximum_fusion.3), channel_id=1, source_target_pairs={{0,4},{4,8},{8,12},{12,16},{16,20},{20,24},{24,28},{1,5},{5,9},{9,... | collective-permute-start | bytes 147464 | tf_op jit(solution)/shard_map/ppermute | solution.py:33
  192.9 1.7 collective-permute-done.7
  195.8 41.9 %all-reduce.74 = (f32[]{:T(128)}, f32[]{:T(128)}) all-reduce(f32[]{:T(128)} %get-tuple-element.221, f32[]{:T(128)} %get-tuple-element.220), channel_id=1, replica_groups=mesh['gx'=8,'gy'=4] {'gx','gy'}, use_global_device_ids=true, to_apply=%region_2.3 | all-reduce | flops 2 | bytes 16 | tf_op jit(solution)/shard_map/psum | solution.py:278
  239.9 39.8 %psum.30 = f32[]{:T(128)} all-reduce(f32[]{:T(128)} %multiply_reduce_fusion), channel_id=1, replica_groups=mesh['gx'=8,'gy'=4] {'gx','gy'}, use_global_device_ids=true, to_apply=%region_9.10 | all-reduce | flops 1 | bytes 8 | tf_op jit(solution)/shard_map/psum | solution.py:278
  283.8 4.9 %collective-permute-done.8 = f32[3,1,32,128]{3,2,1,0:T(8,128)S(1)} collective-permute-done((f32[3,1,32,128]{3,2,1,0:T(8,128)S(1)}, f32[3,1,32,128]{3,2,1,0:T(8,128)S(1)}, u32[]{:S(2)}, u32[]{:S(2)}) %collective-permute-start.8) | collective-permute-done | bytes 49184 | tf_op jit(solution)/shard_map/ppermute | solution.py:33
  293.1 27.3 %while.27 = (s32[]{:T(128)}, f32[4,3,5,33,128]{4,3,2,1,0:T(8,128)}, s32[4]{0:T(128)S(1)}, f32[3,17,33,128]{3,2,1,0:T(8,128)S(1)}, f32[16,32,128]{2,1,0:T(8,128)}...) while((s32[]{:T(128)}, f32[4,3,5,33,128]{4,3,2,1,0:T(8,128)}, ...), condition=%wide.region_11.12_spmd.clone, body=%wide.region_10.11_spmd.sunk.clone.sunk | while | flops 114082952 | bytes 21380648 | solution.py:203
  295.0 2.2 fusion.156
  301.8 2.2 fusion.156
  308.6 2.2 fusion.156
  315.4 2.2 fusion.156
  323.6 4.7 %collective-permute-start.10 = (f32[3,17,1,128]{3,2,1,0:T(1,128)S(1)}, f32[3,17,1,128]{3,2,1,0:T(1,128)S(1)}, u32[]{:S(2)}, u32[]{:S(2)}) collective-permute-start(f32[3,17,1,128]{3,2,1,0:T(1,128)S(1)} %slice.906), channel_id=1, source_target_pairs={{0,1},{1,2},{2,3},{4,5},{5,6},{6,7},{8,9},{9,10},{10,11},{12,13},{... | collective-permute-start | bytes 78344 | tf_op jit(solution)/shard_map/ppermute | solution.py:33
  329.2 4.2 %collective-permute-start.11 = (f32[3,1,32,128]{3,2,1,0:T(8,128)S(1)}, f32[3,1,32,128]{3,2,1,0:T(8,128)S(1)}, u32[]{:S(2)}, u32[]{:S(2)}) collective-permute-start(f32[3,1,32,128]{3,2,1,0:T(8,128)S(1)} %pad_maximum_fusion.2), channel_id=1, source_target_pairs={{0,4},{4,8},{8,12},{12,16},{16,20},{20,24},{24,28},{1,5},{5,9},{9,... | collective-permute-start | bytes 147464 | tf_op jit(solution)/shard_map/ppermute | solution.py:33
  336.8 41.9 %psum.31 = f32[]{:T(128)} all-reduce(f32[]{:T(128)} %fusion.18), channel_id=1, replica_groups=mesh['gx'=8,'gy'=4] {'gx','gy'}, use_global_device_ids=true, to_apply=%region_14.15 | all-reduce | flops 1 | bytes 8 | tf_op jit(solution)/shard_map/psum | solution.py:293
  (269 shorter events, 69.3 us)
Async XLA Ops:
  0.6 1.9 copy-start
  0.6 6.8 %copy-start.14 = (f32[3,128,128]{2,1,0:T(8,128)S(1)}, f32[3,128,128]{2,1,0:T(8,128)}, u32[]{:S(2)}) copy-start(f32[3,128,128]{2,1,0:T(8,128)} %param.19) | copy-start | bytes 589828
  8.1 0.7 copy-start.17
  13.9 14.7 %copy-start.16 = (s32[512,3]{0,1:T(4,128)S(1)}, s32[512,3]{0,1:T(4,128)}, u32[]{:S(2)}) copy-start(s32[512,3]{0,1:T(4,128)} %param.16) | copy-start | bytes 18436
  13.9 14.8 %copy-start.2 = (f32[24,24]{1,0:T(8,128)S(1)}, f32[24,24]{1,0:T(8,128)}, u32[]{:S(2)}) copy-start(f32[24,24]{1,0:T(8,128)} %constant.145.clone) | copy-start | bytes 6916
  22.1 12.2 %copy-start.13 = (f32[3,16,32,128]{3,2,1,0:T(8,128)S(1)}, f32[3,16,32,128]{3,2,1,0:T(8,128)}, u32[]{:S(2)}) copy-start(f32[3,16,32,128]{3,2,1,0:T(8,128)} %param.14) | copy-start | bytes 2359300
  22.2 7.3 %collective-permute-start = (f32[2,32,128]{2,1,0:T(8,128)S(1)}, f32[2,32,128]{2,1,0:T(8,128)S(1)}, u32[]{:S(2)}, u32[]{:S(2)}) collective-permute-start(f32[2,32,128]{2,1,0:T(8,128)S(1)} %get-tuple-element.314), channel_id=1, source_target_pairs={{0,4},{4,8},{8,12},{12,16},{16,20},{20,24},{24,28},{1,5},{5,9},{9,... | collective-permute-start | bytes 98312 | tf_op jit(solution)/shard_map/ppermute | solution.py:24
  27.1 5.8 %collective-permute-start.1 = (f32[2,32,128]{2,1,0:T(8,128)S(1)}, f32[2,32,128]{2,1,0:T(8,128)S(1)}, u32[]{:S(2)}, u32[]{:S(2)}) collective-permute-start(f32[2,32,128]{2,1,0:T(8,128)S(1)} %get-tuple-element.313), channel_id=1, source_target_pairs={{4,0},{8,4},{12,8},{16,12},{20,16},{24,20},{28,24},{5,1},{9,5},{13... | collective-permute-start | bytes 98312 | tf_op jit(solution)/shard_map/ppermute | solution.py:25
  33.0 96.2 %collective-permute-start.2 = (f32[20,2,128]{2,1,0:T(2,128)S(1)}, f32[20,2,128]{2,1,0:T(2,128)S(1)}, u32[]{:S(2)}, u32[]{:S(2)}) collective-permute-start(f32[20,2,128]{2,1,0:T(2,128)S(1)} %get-tuple-element.311), channel_id=1, source_target_pairs={{0,1},{1,2},{2,3},{4,5},{5,6},{6,7},{8,9},{9,10},{10,11},{12,13},{... | collective-permute-start | bytes 61448 | tf_op jit(solution)/shard_map/ppermute | solution.py:24
  34.3 16.5 %copy-start.15 = (f32[3,512]{1,0:T(4,128)S(1)}, f32[3,512]{1,0:T(4,128)}, u32[]{:S(2)}) copy-start(f32[3,512]{1,0:T(4,128)} %param.17) | copy-start | bytes 18436
  127.7 3.1 collective-permute-start.3
  137.0 3.0 copy-start.11
  137.0 1.2 copy-start.7
  140.0 6.0 %collective-permute-start.4 = (f32[3,1,32,128]{3,2,1,0:T(8,128)S(1)}, f32[3,1,32,128]{3,2,1,0:T(8,128)S(1)}, u32[]{:S(2)}, u32[]{:S(2)}) collective-permute-start(f32[3,1,32,128]{3,2,1,0:T(8,128)S(1)} %slice.900), channel_id=1, source_target_pairs={{4,0},{8,4},{12,8},{16,12},{20,16},{24,20},{28,24},{5,1},{9,5},{13... | collective-permute-start | bytes 147464 | tf_op jit(solution)/shard_map/ppermute | solution.py:33
  146.0 5.1 %collective-permute-start.5 = (f32[3,17,1,128]{3,2,1,0:T(1,128)S(1)}, f32[3,17,1,128]{3,2,1,0:T(1,128)S(1)}, u32[]{:S(2)}, u32[]{:S(2)}) collective-permute-start(f32[3,17,1,128]{3,2,1,0:T(1,128)S(1)} %pad_maximum_fusion.5), channel_id=1, source_target_pairs={{1,0},{2,1},{3,2},{5,4},{6,5},{7,6},{9,8},{10,9},{11,10},{13,12},{... | collective-permute-start | bytes 78344 | tf_op jit(solution)/shard_map/ppermute | solution.py:33
  182.9 11.8 %copy-start.5 = (f32[3,16,32,128]{3,2,1,0:T(8,128)S(1)}, f32[3,16,32,128]{3,2,1,0:T(8,128)}, u32[]{:S(2)}) copy-start(f32[3,16,32,128]{3,2,1,0:T(8,128)} %get-tuple-element.247) | copy-start | bytes 2359300
  182.9 11.8 %copy-start.8 = (s32[3,16,32,128]{3,2,1,0:T(8,128)S(1)}, s32[3,16,32,128]{3,2,1,0:T(8,128)}, u32[]{:S(2)}) copy-start(s32[3,16,32,128]{3,2,1,0:T(8,128)} %param.15) | copy-start | bytes 2359300
  182.9 5.4 %collective-permute-start.6 = (f32[3,17,1,128]{3,2,1,0:T(1,128)S(1)}, f32[3,17,1,128]{3,2,1,0:T(1,128)S(1)}, u32[]{:S(2)}, u32[]{:S(2)}) collective-permute-start(f32[3,17,1,128]{3,2,1,0:T(1,128)S(1)} %slice.902), channel_id=1, source_target_pairs={{0,1},{1,2},{2,3},{4,5},{5,6},{6,7},{8,9},{9,10},{10,11},{12,13},{... | collective-permute-start | bytes 78344 | tf_op jit(solution)/shard_map/ppermute | solution.py:33
  188.4 6.3 %collective-permute-start.7 = (f32[3,1,32,128]{3,2,1,0:T(8,128)S(1)}, f32[3,1,32,128]{3,2,1,0:T(8,128)S(1)}, u32[]{:S(2)}, u32[]{:S(2)}) collective-permute-start(f32[3,1,32,128]{3,2,1,0:T(8,128)S(1)} %pad_maximum_fusion.3), channel_id=1, source_target_pairs={{0,4},{4,8},{8,12},{12,16},{16,20},{20,24},{24,28},{1,5},{5,9},{9,... | collective-permute-start | bytes 147464 | tf_op jit(solution)/shard_map/ppermute | solution.py:33
  194.7 44.3 %copy-start.6 = (f32[3,16,32,128]{3,2,1,0:T(8,128)S(1)}, f32[3,16,32,128]{3,2,1,0:T(8,128)}, u32[]{:S(2)}) copy-start(f32[3,16,32,128]{3,2,1,0:T(8,128)} %get-tuple-element.246) | copy-start | bytes 2359300
  195.8 83.9 %copy-start.10 = (f32[3,16,32,128]{3,2,1,0:T(8,128)}, f32[3,16,32,128]{3,2,1,0:T(8,128)S(1)}, u32[]{:S(2)}) copy-start(f32[3,16,32,128]{3,2,1,0:T(8,128)S(1)} %get-tuple-element.244) | copy-start | bytes 2359300
  282.5 10.6 %copy-start.3 = (f32[3,16,32,128]{3,2,1,0:T(8,128)}, f32[3,16,32,128]{3,2,1,0:T(8,128)S(1)}, u32[]{:S(2)}) copy-start(f32[3,16,32,128]{3,2,1,0:T(8,128)S(1)} %multiply_add_fusion.1) | copy-start | bytes 2359300
  282.5 6.2 %collective-permute-start.8 = (f32[3,1,32,128]{3,2,1,0:T(8,128)S(1)}, f32[3,1,32,128]{3,2,1,0:T(8,128)S(1)}, u32[]{:S(2)}, u32[]{:S(2)}) collective-permute-start(f32[3,1,32,128]{3,2,1,0:T(8,128)S(1)} %slice.904), channel_id=1, source_target_pairs={{4,0},{8,4},{12,8},{16,12},{20,16},{24,20},{28,24},{5,1},{9,5},{13... | collective-permute-start | bytes 147464 | tf_op jit(solution)/shard_map/ppermute | solution.py:33
  288.8 3.1 collective-permute-start.9
  323.6 11.5 %copy-start.4 = (f32[3,16,32,128]{3,2,1,0:T(8,128)S(1)}, f32[3,16,32,128]{3,2,1,0:T(8,128)}, u32[]{:S(2)}) copy-start(f32[3,16,32,128]{3,2,1,0:T(8,128)} %copy-done.3) | copy-start | bytes 2359300
  323.6 11.5 %copy-start.9 = (s32[3,16,32,128]{3,2,1,0:T(8,128)S(1)}, s32[3,16,32,128]{3,2,1,0:T(8,128)}, u32[]{:S(2)}) copy-start(s32[3,16,32,128]{3,2,1,0:T(8,128)} %param.15) | copy-start | bytes 2359300
  323.6 5.5 %collective-permute-start.10 = (f32[3,17,1,128]{3,2,1,0:T(1,128)S(1)}, f32[3,17,1,128]{3,2,1,0:T(1,128)S(1)}, u32[]{:S(2)}, u32[]{:S(2)}) collective-permute-start(f32[3,17,1,128]{3,2,1,0:T(1,128)S(1)} %slice.906), channel_id=1, source_target_pairs={{0,1},{1,2},{2,3},{4,5},{5,6},{6,7},{8,9},{9,10},{10,11},{12,13},{... | collective-permute-start | bytes 78344 | tf_op jit(solution)/shard_map/ppermute | solution.py:33
  329.2 6.9 %copy-start.12 = (f32[17,33,128]{2,1,0:T(8,128)S(1)}, f32[17,33,128]{2,1,0:T(8,128)}, u32[]{:S(2)}) copy-start(f32[17,33,128]{2,1,0:T(8,128)} %get-tuple-element.249) | copy-start | bytes 861700
  329.2 5.9 %collective-permute-start.11 = (f32[3,1,32,128]{3,2,1,0:T(8,128)S(1)}, f32[3,1,32,128]{3,2,1,0:T(8,128)S(1)}, u32[]{:S(2)}, u32[]{:S(2)}) collective-permute-start(f32[3,1,32,128]{3,2,1,0:T(8,128)S(1)} %pad_maximum_fusion.2), channel_id=1, source_target_pairs={{0,4},{4,8},{8,12},{12,16},{16,20},{20,24},{24,28},{1,5},{5,9},{9,... | collective-permute-start | bytes 147464 | tf_op jit(solution)/shard_map/ppermute | solution.py:33
  335.1 45.8 %copy-start.1 = (f32[3,64]{1,0:T(4,128)S(1)}, f32[3,64]{1,0:T(4,128)}, u32[]{:S(2)}) copy-start(f32[3,64]{1,0:T(4,128)} %param.18) | copy-start | bytes 2308
where the time goes:
time: 385 us; the launch traced here: 381 us
  blocking collectives  124 us (32%)
  other arithmetic  82.3 us (21%)
  local copies, waits for them, and re-layouts  81.6 us (21%)
  starting transfers between devices  32.4 us (8%)
  matrix products  24.3 us (6%)
  waiting for transfers between devices  24.3 us (6%)
  loops' own time  6.68 us (2%)
  between operations  5.74 us (1%)
    psum x2, blocking collectives, scaled_norm(): return lax.psum(jnp.sum(residual_now * scaled_now), ('gx', 'gy'))  81.7 us
    scatter-add x1, other arithmetic, per_device(): body_force.at[:, index_x, index_y, load_nodes[:, 2]]  57.2 us
    psum x1, blocking collectives, per_device(): alpha = norm_now / lax.psum(jnp.sum(direction * image), ('gx', 'gy'))  41.9 us
    ppermute x8, starting transfers between devices, shifted(): lax.ppermute(value, axis, [(source, source + steps) for source in range(l...  23.4 us
    ppermute x8, waiting for transfers between devices, shifted(): lax.ppermute(value, axis, [(source, source + steps) for source in range(l...  19.9 us
    scatter-add x1, local copies, waits for them, and re-layouts, per_device(): body_force.at[:, index_x, index_y, load_nodes[:, 2]]  19.5 us
    dot_general x8, matrix products, corner_products(): jnp.dot(stiffness, stacked, precision=highest, preferred_element_type=jnp...  17.5 us
    unnamed x40, local copies, waits for them, and re-layouts  17.5 us
  transfers between devices with their start and end apart: 12, of which 10 were waited for; matrix products, arithmetic and copies ran while one was open for 25% of the time, Pallas kernels for 0%

commit v1 on v0

v1 whole, which is shorter than its diff:
```python
import functools
import math

import jax
import jax.numpy as jnp
from jax import lax
from jax.experimental import pallas as pl
from jax.experimental.pallas import tpu as pltpu
from jax.sharding import PartitionSpec as P

MESH = pl.DeviceIdType.MESH
CF = 4
HALO = 2
f32 = jnp.float32
bf16 = jnp.bfloat16
POISSON = 0.3
LAM = POISSON / ((1.0 + POISSON) * (1.0 - 2.0 * POISSON))
MU = 1.0 / (2.0 * (1.0 + POISSON))
TWO_PI = 2.0 * math.pi
DIAG = ((LAM + 4.0 * MU) * (1.0 + 2.0 / 3.0 + 1.0 / 9.0)) / 16.0
FULL = pl.BlockSpec(memory_space=pltpu.VMEM)


def halo_kernel(bf, fx, xb, xf, yh, ch, ys, send, recv):
    gx, gy = lax.axis_index("gx"), lax.axis_index("gy")
    nx, ny = lax.axis_size("gx"), lax.axis_size("gy")
    planes, rows = bf.shape[1], bf.shape[2]

    def at(dx, dy):
        return (lax.rem(gx + dx + nx, nx), lax.rem(gy + dy + ny, ny))

    barrier = pltpu.get_barrier_semaphore()
    around = [(dx, dy) for dx in (-1, 0, 1) for dy in (-1, 0, 1) if dx or dy]
    for dx, dy in around:
        pl.semaphore_signal(barrier, inc=1, device_id=at(dx, dy), device_id_type=MESH)
    for side in range(2):
        first = 0 if side == 0 else rows - HALO
        for c in range(3):
            span = slice(HALO * c, HALO * c + HALO)
            ys[side, :, 0, span, :] = bf[c, :, first : first + HALO, :]
            ys[side, :, 1, span, :] = 1.0 - fx[c, :, first : first + HALO, :].astype(f32)
        ys[side, :, :, 3 * HALO :, :] = jnp.zeros((planes, 2, 8 - 3 * HALO, bf.shape[3]), f32)
    pl.semaphore_wait(barrier, len(around))
    copies = []

    def launch(src, dst, where):
        index = len(copies)
        copy = pltpu.make_async_remote_copy(
            src_ref=src,
            dst_ref=dst,
            send_sem=send.at[index],
            recv_sem=recv.at[index],
            device_id=where,
            device_id_type=MESH,
        )
        copy.start()
        copies.append(copy)

    for side in range(2):
        step = 2 * side - 1
        near = pl.ds(0 if side == 0 else planes - HALO, HALO)
        launch(bf.at[:, near], xb.at[1 - side], at(step, 0))
        launch(fx.at[:, near], xf.at[1 - side], at(step, 0))
        launch(ys.at[side], yh.at[1 - side], at(0, step))
        for other in range(2):
            launch(
                ys.at[other, near], ch.at[1 - side, 1 - other], at(step, 2 * other - 1)
            )
    for copy in copies:
        copy.wait()


def sum_kernel(mine, total, along, across, part, send, recv):
    gx, gy = lax.axis_index("gx"), lax.axis_index("gy")
    nx, ny = lax.axis_size("gx"), lax.axis_size("gy")
    barrier = pltpu.get_barrier_semaphore()
    for k in range(1, nx):
        pl.semaphore_signal(
            barrier, inc=1, device_id=(lax.rem(gx + k, nx), gy), device_id_type=MESH
        )
    for k in range(1, ny):
        pl.semaphore_signal(
            barrier, inc=1, device_id=(gx, lax.rem(gy + k, ny)), device_id_type=MESH
        )
    pl.semaphore_wait(barrier, nx + ny - 2)

    def exchange(src, dst, count, base, where):
        copies = []
        for k in range(1, count):
            copy = pltpu.make_async_remote_copy(
                src_ref=src,
                dst_ref=dst.at[k - 1],
                send_sem=send.at[base + k - 1],
                recv_sem=recv.at[base + k - 1],
                device_id=where(k),
                device_id_type=MESH,
            )
            copy.start()
            copies.append(copy)
        for copy in copies:
            copy.wait()

    exchange(mine, along, nx, 0, lambda k: (lax.rem(gx + k, nx), gy))
    part[...] = mine[...] + jnp.sum(along[...], axis=0)
    exchange(part, across, ny, nx - 1, lambda k: (gx, lax.rem(gy + k, ny)))
    total[...] = part[...] + jnp.sum(across[...], axis=0)


def split(value):
    high = value.astype(bf16)
    return high, (value - high.astype(f32)).astype(bf16)


def work_kernel(
    bf, fx, xb, xf, yh, ch, nodes, loads, freq, hw, hb, ow, ob,
    z_out, q_out, dens, sums,
    wide, up, filt, ye, inv_s, force, free_s, z_s, q_s,
):
    gx, gy = lax.axis_index("gx"), lax.axis_index("gy")
    nx, ny = lax.axis_size("gx"), lax.axis_size("gy")
    planes, rows, height = bf.shape[1], bf.shape[2], bf.shape[3]
    cx, cy, cz = planes // CF + 2, rows // CF + 2, height // CF
    tall = cy * CF
    deep = planes + 2 * HALO
    total_cx, total_cy = nx * (planes // CF), ny * (rows // CF)
    plane = (tall, height)
    lane = lax.broadcasted_iota(jnp.int32, plane, 1)
    row = lax.broadcasted_iota(jnp.int32, plane, 0)
    own_row = ((row >= CF) & (row < CF + rows)).astype(f32)
    cell_row = gy * rows - CF + row
    inside_y = ((cell_row >= 0) & (cell_row < ny * rows)).astype(f32)

    def up_z(v):
        return jnp.where(lane < height - 1, pltpu.roll(v, height - 1, 1), 0.0)

    def down_z(v):
        return jnp.where(lane > 0, pltpu.roll(v, 1, 1), 0.0)

    def up_y(v):
        return pltpu.roll(v, tall - 1, 0)

    def down_y(v):
        return pltpu.roll(v, 1, 0)

    def fold(v):
        return jnp.sum(v.reshape(tall // 8, 8, height), axis=0)

    layers, width = hw.shape[0], hw.shape[2]
    for layer in range(layers):
        high, low = split(hw[layer])
        both = jnp.concatenate([high, low], axis=1)
        wide[layer] = jnp.concatenate([both, both], axis=0)
    high, low = split(jnp.broadcast_to(ow[...], (height, width)))
    wide_out = jnp.concatenate(
        [jnp.concatenate([high, high], axis=1), jnp.concatenate([low, low], axis=1)], axis=0
    )
    turn = jnp.concatenate([freq[...], freq[...]], axis=1)
    half = freq.shape[1]

    def index_rows(count):
        return lax.broadcasted_iota(jnp.int32, (count, 2 * half), 0)

    def wave(t):
        t = (t - jnp.floor(t + 0.5)) * TWO_PI
        return jnp.sin(t), jnp.cos(t)

    quarter = (lax.broadcasted_iota(jnp.int32, (1, 2 * half), 1) >= half).astype(f32) * 0.25
    at_z = (index_rows(cz).astype(f32) + 0.5) / float(cz)
    sin_v, cos_v = wave(at_z * turn[2:3])
    padded_cy = -(-cy // 8) * 8
    at_y = ((gy * (rows // CF) - 1 + index_rows(padded_cy)).astype(f32) + 0.5) / float(total_cy)
    turn_y = at_y * turn[1:2]
    pick = (
        lax.broadcasted_iota(jnp.int32, (cz, height), 1) // CF
        == lax.broadcasted_iota(jnp.int32, (cz, height), 0)
    ).astype(f32)
    bias_out = ob[0, 0]

    def cells(ix, _):
        index_x = gx * (planes // CF) - 1 + ix
        inside_x = jnp.where((index_x >= 0) & (index_x < total_cx), 1.0, 0.0).astype(f32)
        at_x = (index_x.astype(f32) + 0.5) / float(total_cx)
        sin_u, cos_u = wave(turn_y + (at_x * turn[0:1] + quarter))
        hidden = jnp.concatenate(
            [sin_u[j : j + 1] * cos_v + cos_u[j : j + 1] * sin_v for j in range(cy)], axis=0
        )
        for layer in range(layers):
            lhs = jnp.concatenate(split(hidden), axis=1)
            out = jnp.dot(lhs, wide[layer], preferred_element_type=f32)
            mixed = out[:, :width] + out[:, width:] + hb[layer : layer + 1, :]
            hidden = mixed / (1.0 + jnp.exp(jnp.minimum(-mixed, 80.0)))
        lhs = jnp.concatenate(split(hidden), axis=1)
        out = lax.dot_general(
            lhs, wide_out, (((1,), (1,)), ((), ())), preferred_element_type=f32
        )
        spread = (out[:, :height] + out[:, height:]).reshape(cy, cz, height)
        logits = jnp.sum(spread * pick[None], axis=1) + bias_out
        coarse = 1.0 / (1.0 + jnp.exp(jnp.minimum(-logits, 80.0)))
        for j in range(cy):
            up[ix, CF * j : CF * j + CF, :] = jnp.broadcast_to(coarse[j : j + 1], (CF, height))
        inside = inside_y * inside_x
        for base, values in ((0, up[ix] * inside), (2, inside)):
            beside = up_z(values) + down_z(values)
            w2, w3 = 2.0 - math.sqrt(2.0), 2.0 - math.sqrt(3.0)
            one = values + w2 * beside
            two = w2 * values + w3 * beside
            filt[base, ix] = 2.0 * values + beside + up_y(one) + down_y(one)
            filt[base + 1, ix] = one + up_y(two) + down_y(two)
        return 0

    lax.fori_loop(0, cx, cells, 0)

    def filtered(i, _):
        here, back, ahead = (i + 1) // CF, i // CF, (i + 2) // CF
        top = filt[0, here] + filt[1, back] + filt[1, ahead]
        bottom = filt[2, here] + filt[3, back] + filt[3, ahead]
        value = top / jnp.maximum(bottom, 0.5)
        index_x = gx * (planes // CF) - 1 + here
        inside_x = jnp.where((index_x >= 0) & (index_x < total_cx), 1.0, 0.0).astype(f32)
        ye[i] = (0.02 + 0.98 * value * value * value) * (inside_y * inside_x)

        @pl.when((i >= HALO + 1) & (i < HALO + 1 + planes))
        def _():
            dens[i - HALO - 1] = value[CF : CF + rows]

        return 0

    lax.fori_loop(0, deep + 1, filtered, 0)

    count = nodes.shape[0]
    eye = (
        lax.broadcasted_iota(jnp.int32, (8, 3), 0) == lax.broadcasted_iota(jnp.int32, (8, 3), 1)
    ).astype(f32)
    flat = lax.dot_general(
        eye,
        nodes[...].astype(f32),
        (((1,), (1,)), ((), ())),
        precision=lax.Precision.HIGHEST,
        preferred_element_type=f32,
    )
    flat = (flat + 0.5).astype(jnp.int32)
    local_x = flat[0:1] - gx * planes + HALO
    local_y = flat[1:2] - gy * rows + CF
    near = (local_x >= 0) & (local_x < deep) & (local_y >= 0) & (local_y < tall)
    place = jnp.where(near, local_x * tall + local_y, -1)
    hit_z = lax.broadcasted_iota(jnp.int32, (height, count), 0) == flat[2:3]
    pieces = [[], [], []]
    for c in range(3):
        rest = loads[c : c + 1, :]
        for term in range(3):
            high = rest.astype(bf16).astype(f32)
            pieces[term].append(jnp.where(hit_z, high, 0.0).astype(bf16))
            rest = rest - high
    table = jnp.concatenate(pieces[0] + pieces[1] + pieces[2], axis=0)
    group = 4

    def place_loads(g, _):
        here = g * (group * tall) + lax.broadcasted_iota(jnp.int32, (group * tall, count), 0)
        hit = jnp.where(here == place, 1.0, 0.0).astype(bf16)
        out = lax.dot_general(hit, table, (((1,), (1,)), ((), ())), preferred_element_type=f32)
        for c in range(3):
            parts = [out[:, (3 * t + c) * height : (3 * t + c + 1) * height] for t in range(3)]
            z_s[c, pl.ds(g * group, group)] = ((parts[2] + parts[1]) + parts[0]).reshape(
                group, tall, height
            )
        return 0

    lax.fori_loop(0, deep // group, place_loads, 0)

    edge = CF - HALO
    for ref in (force, free_s):
        ref[:, :, :edge, :] = jnp.zeros((3, deep, edge, height), f32)
        ref[:, :, tall - edge :, :] = jnp.zeros((3, deep, edge, height), f32)
    own = slice(CF, CF + rows)
    force[:, HALO : HALO + planes, own] = bf[...]
    free_s[:, HALO : HALO + planes, own] = 1.0 - fx[...].astype(f32)
    for side in range(2):
        first = 0 if side == 0 else deep - HALO
        force[:, first : first + HALO, own] = xb[side]
        free_s[:, first : first + HALO, own] = 1.0 - xf[side].astype(f32)
        start = edge if side == 0 else CF + rows
        for c in range(3):
            span = slice(HALO * c, HALO * c + HALO)
            for ref, which in ((force, 0), (free_s, 1)):
                ref[c, HALO : HALO + planes, start : start + HALO] = yh[side, :, which, span]
                for other in range(2):
                    begin = 0 if other == 0 else deep - HALO
                    ref[c, begin : begin + HALO, start : start + HALO] = ch[
                        other, side, :, which, span
                    ]
    node_row = gy * rows - CF + row
    in_y = ((node_row >= 0) & (node_row < ny * rows)).astype(f32)

    def own_plane(m):
        return jnp.where((m >= HALO) & (m < HALO + planes), 1.0, 0.0).astype(f32)

    def begin(m, total):
        node_x = gx * planes - HALO + m
        in_x = jnp.where((node_x >= 0) & (node_x < nx * planes), 1.0, 0.0).astype(f32)
        s = ye[m] + ye[m + 1]
        s = s + down_y(s)
        s = s + down_z(s)
        inv = 1.0 / jnp.maximum(DIAG * s, 1e-4)
        inv_s[m] = inv
        counted = own_row * own_plane(m)
        inside = in_y * in_x
        part = jnp.zeros(plane, f32)
        for c in range(3):
            free = free_s[c, m] * inside
            free_s[c, m] = free
            rhs = free * (force[c, m] + z_s[c, m])
            z0 = rhs * inv
            z_s[c, m] = z0
            part = part + rhs * z0
        return total + fold(part * counted)

    zero = jnp.zeros((8, height), f32)
    sum_a = lax.fori_loop(0, deep, begin, zero)

    def element_forces(src, e):
        modes = []
        for c in range(3):
            low, high = src[c, e], src[c, e + 1]
            by = {}
            for name_x, v in (("S", low + high), ("D", high - low)):
                w = up_y(v)
                for name_y, t in (("S", v + w), ("D", w - v)):
                    u = up_z(t)
                    if name_x + name_y != "SS":
                        by[name_x + name_y + "S"] = t + u
                    by[name_x + name_y + "D"] = u - t
            modes.append(by)
        x, y, z = modes
        y1 = ye[e + 1] * (1.0 / 16.0)
        y3 = y1 * (1.0 / 3.0)
        out = ({}, {}, {})
        trace = LAM * (x["DSS"] + y["SDS"] + z["SSD"])
        out[0]["DSS"] = y1 * (trace + (2 * MU) * x["DSS"])
        out[1]["SDS"] = y1 * (trace + (2 * MU) * y["SDS"])
        out[2]["SSD"] = y1 * (trace + (2 * MU) * z["SSD"])
        ym = y1 * MU
        out[0]["SDS"] = out[1]["DSS"] = ym * (x["SDS"] + y["DSS"])
        out[0]["SSD"] = out[2]["DSS"] = ym * (x["SSD"] + z["DSS"])
        out[1]["SSD"] = out[2]["SDS"] = ym * (y["SSD"] + z["SDS"])
        t = LAM * (y["DDS"] + z["DSD"])
        out[1]["DDS"] = y3 * (t + (3 * MU) * y["DDS"])
        out[2]["DSD"] = y3 * (t + (3 * MU) * z["DSD"])
        t = LAM * (x["DDS"] + z["SDD"])
        out[0]["DDS"] = y3 * (t + (3 * MU) * x["DDS"])
        out[2]["SDD"] = y3 * (t + (3 * MU) * z["SDD"])
        t = LAM * (x["DSD"] + y["SDD"])
        out[0]["DSD"] = y3 * (t + (3 * MU) * x["DSD"])
        out[1]["SDD"] = y3 * (t + (3 * MU) * y["SDD"])
        ym = y3 * MU
        p, q, r = y["DSD"], z["DDS"], x["SDD"]
        out[1]["DSD"] = ym * ((p + q) + (r + p))
        out[2]["DDS"] = ym * ((p + q) + (r + q))
        out[0]["SDD"] = ym * ((r + q) + (r + p))
        y9 = y1 * ((LAM + 4.0 * MU) / 9.0)
        for c in range(3):
            out[c]["DDD"] = y9 * modes[c]["DDD"]
        lows, highs = [], []
        for c in range(3):
            by_x = []
            for name_x in "SD":
                by_y = []
                for name_y in "SD":
                    d = out[c][name_x + name_y + "D"]
                    if name_x + name_y == "SS":
                        by_y.append(down_z(d) - d)
                    else:
                        s = out[c][name_x + name_y + "S"]
                        by_y.append((s - d) + down_z(s + d))
                s, d = by_y
                by_x.append((s - d) + down_y(s + d))
            s, d = by_x
            lows.append(s - d)
            highs.append(s + d)
        return lows, highs

    def first(e, carry):
        c0, c1, c2, sum_b, sum_c = carry
        lows, highs = element_forces(z_s, e)
        inv = inv_s[e]
        counted = own_row * own_plane(e)
        part_b = jnp.zeros(plane, f32)
        part_c = jnp.zeros(plane, f32)
        for c, before in enumerate((c0, c1, c2)):
            w = free_s[c, e] * (before + lows[c])
            q = w * inv
            q_s[c, e] = q
            part_b = part_b + w * z_s[c, e]
            part_c = part_c + w * q
        return (*highs, sum_b + fold(part_b * counted), sum_c + fold(part_c * counted))

    blank = jnp.zeros(plane, f32)
    *_, sum_b, sum_c = lax.fori_loop(0, deep - 1, first, (blank, blank, blank, zero, zero))

    def second(e, carry):
        c0, c1, c2, sum_d = carry
        lows, highs = element_forces(q_s, e)
        counted = own_row * own_plane(e)
        part = jnp.zeros(plane, f32)
        for c, before in enumerate((c0, c1, c2)):
            part = part + free_s[c, e] * (before + lows[c]) * q_s[c, e]
        return (*highs, sum_d + fold(part * counted))

    *_, sum_d = lax.fori_loop(1, HALO + planes, second, (blank, blank, blank, zero))
    z_out[...] = z_s[:, HALO : HALO + planes, own]
    q_out[...] = q_s[:, HALO : HALO + planes, own]
    sums[...] = jnp.zeros_like(sums)
    for index, value in enumerate((sum_a, sum_b, sum_c, sum_d)):
        sums[index : index + 1, :] = jnp.sum(value, axis=0, keepdims=True)


def per_device(bf, fx, nodes, loads, freq, hw, hb, ow, ob):
    nx, ny = lax.axis_size("gx"), lax.axis_size("gy")
    _, planes, rows, height = bf.shape
    shape = jax.ShapeDtypeStruct
    halo = (2, 3, HALO, rows, height)
    packed = (2, planes, 2, 8, height)
    corner = (2, 2, HALO, 2, 8, height)
    xb, xf, yh, ch = pl.pallas_call(
        halo_kernel,
        out_shape=[
            shape(halo, f32), shape(halo, jnp.int32), shape(packed, f32), shape(corner, f32)
        ],
        in_specs=[FULL] * 2,
        out_specs=[FULL] * 4,
        scratch_shapes=[
            pltpu.VMEM(packed, f32),
            pltpu.SemaphoreType.DMA((10,)),
            pltpu.SemaphoreType.DMA((10,)),
        ],
        compiler_params=pltpu.CompilerParams(
            collective_id=0, has_side_effects=True, vmem_limit_bytes=16 << 20
        ),
    )(bf, fx)
    cx, tall, deep = planes // CF + 2, rows + 2 * CF, planes + 2 * HALO
    width = hw.shape[2]
    field = pltpu.VMEM((3, deep, tall, height), f32)
    z0, q, density, sums = pl.pallas_call(
        work_kernel,
        out_shape=[
            shape(bf.shape, f32),
            shape(bf.shape, f32),
            shape(bf.shape[1:], f32),
            shape((8, height), f32),
        ],
        in_specs=[FULL] * 12 + [pl.BlockSpec(memory_space=pltpu.SMEM)],
        out_specs=[FULL] * 4,
        scratch_shapes=[
            pltpu.VMEM((hw.shape[0], 2 * width, 2 * width), bf16),
            pltpu.VMEM((cx, tall, height), f32),
            pltpu.VMEM((4, cx, tall, height), f32),
            pltpu.VMEM((deep + 1, tall, height), f32),
            pltpu.VMEM((deep, tall, height), f32),
            field,
            field,
            field,
            field,
        ],
        compiler_params=pltpu.CompilerParams(vmem_limit_bytes=40 << 20),
    )(bf, fx, xb, xf, yh, ch, nodes, loads, freq, hw, hb, ow.reshape(1, -1), ob.reshape(1, 1))
    total = pl.pallas_call(
        sum_kernel,
        out_shape=shape(sums.shape, f32),
        in_specs=[FULL],
        out_specs=FULL,
        scratch_shapes=[
            pltpu.VMEM((nx - 1, *sums.shape), f32),
            pltpu.VMEM((ny - 1, *sums.shape), f32),
            pltpu.VMEM(sums.shape, f32),
            pltpu.SemaphoreType.DMA((nx + ny - 2,)),
            pltpu.SemaphoreType.DMA((nx + ny - 2,)),
        ],
        compiler_params=pltpu.CompilerParams(
            collective_id=1, has_side_effects=True, vmem_limit_bytes=16 << 20
        ),
    )(sums)
    scalars = jnp.sum(total, axis=1)
    a, b, c, d = (scalars[i] for i in range(4))
    alpha = a / b
    next_rz = a - 2.0 * alpha * b + alpha * alpha * c
    beta = next_rz / a
    bent = b - 2.0 * alpha * c + alpha * alpha * d
    energy = bent + 2.0 * beta * (b - alpha * c) + beta * beta * b
    alpha_next = next_rz / energy
    along_z = alpha + alpha_next * (1.0 + beta)
    displacement = along_z * z0 - (alpha_next * alpha) * q
    return displacement, density


def solution(mesh):
    grid = P(None, "gx", "gy", None)
    return jax.shard_map(
        per_device,
        mesh=mesh,
        in_specs=(grid, grid, P(), P(), P(), P(), P(), P(), P()),
        out_specs=(grid, P("gx", "gy", None)),
        check_vma=False,
    )
```

time: 385 us -> 63.4 us (0.16)
  blocking collectives: 124 us -> 0 us
  other arithmetic: 82.3 us -> 1.16 us
  local copies, waits for them, and re-layouts: 81.6 us -> 4.43 us
  Pallas kernels: 0 us -> 48.4 us
  starting transfers between devices: 32.4 us -> 0 us
  matrix products: 24.3 us -> 0 us
  waiting for transfers between devices: 24.3 us -> 0 us
  loops' own time: 6.68 us -> 0 us
    psum x3 -> x0, blocking collectives: 124 us -> none  [the longest x2 81.7 us: scaled_norm(): return lax.psum(jnp.sum(residual_now * scaled_now), ('gx', 'gy'))]
    scatter-add x3 -> x0, other arithmetic: 58.9 us -> none  [the longest x1 57.2 us: per_device(): body_force.at[:, index_x, index_y, load_nodes[:, 2]]]
    pallas_call x0 -> x3, Pallas kernels: none -> 48.4 us  [the longest x1 22.3 us: per_device(): pl.pallas_call(work_kernel, out_shape=[shape(bf.shape, f32), shape(bf.sha...]
    ppermute x12 -> x0, starting transfers between devices: 32.4 us -> none  [the longest x8 23.4 us: shifted(): lax.ppermute(value, axis, [(source, source + steps) for source in range(l...]
    ppermute x12 -> x0, waiting for transfers between devices: 24.3 us -> none  [the longest x8 19.9 us: shifted(): lax.ppermute(value, axis, [(source, source + steps) for source in range(l...]
    dot_general x13 -> x0, matrix products: 24.3 us -> none  [the longest x8 17.5 us: corner_products(): jnp.dot(stiffness, stacked, precision=highest, preferred_element_type=jnp...]
    scatter-add x1 -> x0, local copies, waits for them, and re-layouts: 19.5 us -> none  [per_device(): body_force.at[:, index_x, index_y, load_nodes[:, 2]]]
    unnamed x40 -> x19, local copies, waits for them, and re-layouts: 17.5 us -> 3.79 us
  transfers between devices with their start and end apart: 12 -> 0, of which waited for: 10 -> 0; matrix products, arithmetic and copies ran while one was open for 25% -> 0% of each run, Pallas kernels for 0% -> 0%
where the time goes in v1:
time: 63.4 us; the launch traced here: 63 us
  Pallas kernels  48.4 us (76%)
  between operations  9.07 us (14%)
  local copies, waits for them, and re-layouts  4.43 us (7%)
  other arithmetic  1.16 us (2%)
    pallas_call x1, Pallas kernels, per_device(): pl.pallas_call(work_kernel, out_shape=[shape(bf.shape, f32), shape(bf.sha...  22.3 us
    pallas_call x1, Pallas kernels, per_device(): pl.pallas_call(halo_kernel, out_shape=[shape(halo, f32), shape(halo, jnp....  16.1 us
    pallas_call x1, Pallas kernels, per_device(): pl.pallas_call(sum_kernel, out_shape=shape(sums.shape, f32), in_specs=[FU...  10 us
    unnamed x19, local copies, waits for them, and re-layouts  3.79 us

profile of v1, /device:TPU:0, one launch (start us, length us, event | category | flops | bytes accessed | tf_op | source)
XLA Modules:
  0.0 63.0 jit_solution(7682830771496059036)
XLA Ops:
  1.3 0.0 copy-start.4
  1.3 0.0 copy-start.5
  1.3 0.9 %copy.11.nodes = s32[512,3]{1,0:T(8,128)S(1)} copy(s32[512,3]{0,1:T(4,128)} %param.11) | data formatting | bytes 12288 | tf_op args[2]
  2.2 0.0 copy-start
  2.2 1.1 %copy-done = f32[3,16,32,128]{3,2,1,0:T(8,128)S(1)} copy-done((f32[3,16,32,128]{3,2,1,0:T(8,128)S(1)}, f32[3,16,32,128]{3,2,1,0:T(8,128)}, u32[]{:S(2)}) %copy-start) | copy-done | bytes 786456
  3.3 0.0 copy-start.2
  3.3 1.1 %copy-done.2 = s32[3,16,32,128]{3,2,1,0:T(8,128)S(1)} copy-done((s32[3,16,32,128]{3,2,1,0:T(8,128)S(1)}, s32[3,16,32,128]{3,2,1,0:T(8,128)}, u32[]{:S(2)}) %copy-start.2) | copy-done | bytes 786456
  4.5 0.0 copy-start.1
  4.5 0.0 copy-start.3
  4.5 16.1 %shard_map.104 = (f32[2,3,2,32,128]{4,3,2,1,0:T(8,128)S(1)}, s32[2,3,2,32,128]{4,3,2,1,0:T(8,128)S(1)}, f32[2,16,2,8,128]{4,3,2,1,0:T(8,128)S(1)}, f32[2,2,2,2,8,128]{5,4,3,2,1,0:T(8,128)S(1)}) custom-call(f32[3,16,32,128]{3,2,1,0:T(8,128)S(1)} %copy-done, s32[3,16,32,128]{3,2,1,0:T(8,128)S(1)} %copy-done.2), custom_call_target="tpu_custom_call" | custom-call | tf_op jit(solution)/shard_map/pallas_call | solution.py:423
  20.5 0.0 copy-start.7
  20.5 0.0 copy-start.6
  20.6 0.0 copy-start.8
  20.6 0.0 copy-done.4
  20.6 0.0 copy-done.5
  20.6 0.0 copy-done.1
  20.6 0.0 copy-done.3
  20.6 0.6 copy-done.7
  21.2 0.0 copy-done.6
  21.2 0.0 copy-done.8
  21.2 22.3 %shard_map.105 = (f32[3,16,32,128]{3,2,1,0:T(8,128)S(1)}, f32[3,16,32,128]{3,2,1,0:T(8,128)S(1)}, f32[16,32,128]{2,1,0:T(8,128)}, f32[8,128]{1,0:T(8,128)S(1)}) custom-call(f32[3,16,32,128]{3,2,1,0:T(8,128)S(1)} %copy-done.1, s32[3,16,32,128]{3,2,1,0:T(8,128)S(1)} %copy-done.3, f32[2,3,2,32,128]{4,3,2,1,0:T(8,128)S(1)} %get-tuple-element.10.xb, ...), custom_call_target="tpu_custom_call" | custom-call | tf_op jit(solution)/shard_map/pallas_call | solution.py:442
  43.5 10.0 %shard_map.106 = f32[8,128]{1,0:T(8,128)S(1)} custom-call(f32[8,128]{1,0:T(8,128)S(1)} %get-tuple-element.14.mine), custom_call_target="tpu_custom_call" | custom-call | tf_op jit(solution)/shard_map/pallas_call | solution.py:465
  53.6 0.1 reduce_sum.9
  53.7 0.6 %fusion = (f32[1]{0:T(128)}, f32[1]{0:T(128)}, f32[1]{0:T(128)}, f32[1]{0:T(128)}) fusion(f32[8]{0:T(128)S(1)} %reduce_sum.9), kind=kLoop, calls=%fused_computation.1 | loop fusion | bytes 32 | tf_op jit(solution)/shard_map/slice | solution.py:482
  62.0 1.0 %multiply_subtract_fusion = f32[3,16,32,128]{3,2,1,0:T(8,128)} fusion(f32[3,16,32,128]{3,2,1,0:T(8,128)S(1)} %get-tuple-element.16, f32[3,16,32,128]{3,2,1,0:T(8,128)S(1)} %get-tuple-element.15, f32[]{:T(128)S(6)} %mul.67, f32[]{:T(128)S(6)} %add.19), kind=kLoop, calls=%fused_computation | loop fusion | flops 589824 | bytes 2359304 | tf_op jit(solution)/shard_map/sub | solution.py:490
Async XLA Ops:
  1.3 19.3 %copy-start.4 = (f32[3,128,128]{2,1,0:T(8,128)S(1)}, f32[3,128,128]{2,1,0:T(8,128)}, u32[]{:S(2)}) copy-start(f32[3,128,128]{2,1,0:T(8,128)} %hw.1) | copy-start | bytes 589828
  1.3 19.3 %copy-start.5 = (f32[3,512]{1,0:T(4,128)S(1)}, f32[3,512]{1,0:T(4,128)}, u32[]{:S(2)}) copy-start(f32[3,512]{1,0:T(4,128)} %loads.1) | copy-start | bytes 18436
  2.2 1.1 %copy-start = (f32[3,16,32,128]{3,2,1,0:T(8,128)S(1)}, f32[3,16,32,128]{3,2,1,0:T(8,128)}, u32[]{:S(2)}) copy-start(f32[3,16,32,128]{3,2,1,0:T(8,128)} %bf.3) | copy-start | bytes 2359300
  3.3 1.1 %copy-start.2 = (s32[3,16,32,128]{3,2,1,0:T(8,128)S(1)}, s32[3,16,32,128]{3,2,1,0:T(8,128)}, u32[]{:S(2)}) copy-start(s32[3,16,32,128]{3,2,1,0:T(8,128)} %fx.3) | copy-start | bytes 2359300
  4.5 16.1 %copy-start.1 = (f32[3,16,32,128]{3,2,1,0:T(8,128)S(1)}, f32[3,16,32,128]{3,2,1,0:T(8,128)}, u32[]{:S(2)}) copy-start(f32[3,16,32,128]{3,2,1,0:T(8,128)} %bf.3) | copy-start | bytes 2359300
  4.5 16.1 %copy-start.3 = (s32[3,16,32,128]{3,2,1,0:T(8,128)S(1)}, s32[3,16,32,128]{3,2,1,0:T(8,128)}, u32[]{:S(2)}) copy-start(s32[3,16,32,128]{3,2,1,0:T(8,128)} %fx.3) | copy-start | bytes 2359300
  20.5 0.7 %copy-start.7 = (f32[3,128]{1,0:T(4,128)S(1)}, f32[3,128]{1,0:T(4,128)}, u32[]{:S(2)}) copy-start(f32[3,128]{1,0:T(4,128)} %hb.1) | copy-start | bytes 4612
  20.5 0.7 %copy-start.6 = (f32[3,64]{1,0:T(4,128)S(1)}, f32[3,64]{1,0:T(4,128)}, u32[]{:S(2)}) copy-start(f32[3,64]{1,0:T(4,128)} %freq.1) | copy-start | bytes 2308
  20.6 0.7 %copy-start.8 = (f32[128]{0:T(128)S(1)}, f32[128]{0:T(128)}, u32[]{:S(2)}) copy-start(f32[128]{0:T(128)} %param.16) | copy-start | bytes 1540

commit v2 on v1

--- a/solution.py
+++ b/solution.py
@@ -21,104 +21,85 @@
 FULL = pl.BlockSpec(memory_space=pltpu.VMEM)
 
 
-def halo_kernel(bf, fx, xb, xf, yh, ch, ys, send, recv):
+def split(value):
+    high = value.astype(bf16)
+    return high, (value - high.astype(f32)).astype(bf16)
+
+
+def whole_kernel(
+    bf_far, fx_far, nodes, loads, freq, hw, hb, ow, ob,
+    x_out, dens,
+    bf, fx, xb, xf, yh, ch, ys, along, across, mine, part,
+    wide, up, filt, ye, inv_s, force, free_s, z_s, q_s,
+    local, send, recv, sum_send, sum_recv,
+):
     gx, gy = lax.axis_index("gx"), lax.axis_index("gy")
     nx, ny = lax.axis_size("gx"), lax.axis_size("gy")
-    planes, rows = bf.shape[1], bf.shape[2]
+    planes, rows, height = bf.shape[1], bf.shape[2], bf.shape[3]
+
+    fetches = []
+    for c in range(3):
+        for far, near, index in ((bf_far, bf, c), (fx_far, fx, 3 + c)):
+            fetch = pltpu.make_async_copy(far.at[c], near.at[c], local.at[index])
+            fetch.start()
+            fetches.append(fetch)
+    for ref in (xb, xf, yh, ch):
+        ref[...] = jnp.zeros_like(ref)
 
     def at(dx, dy):
         return (lax.rem(gx + dx + nx, nx), lax.rem(gy + dy + ny, ny))
 
     barrier = pltpu.get_barrier_semaphore()
-    around = [(dx, dy) for dx in (-1, 0, 1) for dy in (-1, 0, 1) if dx or dy]
-    for dx, dy in around:
-        pl.semaphore_signal(barrier, inc=1, device_id=at(dx, dy), device_id_type=MESH)
-    for side in range(2):
-        first = 0 if side == 0 else rows - HALO
-        for c in range(3):
-            span = slice(HALO * c, HALO * c + HALO)
-            ys[side, :, 0, span, :] = bf[c, :, first : first + HALO, :]
-            ys[side, :, 1, span, :] = 1.0 - fx[c, :, first : first + HALO, :].astype(f32)
-        ys[side, :, :, 3 * HALO :, :] = jnp.zeros((planes, 2, 8 - 3 * HALO, bf.shape[3]), f32)
-    pl.semaphore_wait(barrier, len(around))
+    partners = [at(dx, dy) for dx in (-1, 1) for dy in (-1, 1)]
+    partners += [at(k, 0) for k in range(1, nx)] + [at(0, k) for k in range(1, ny)]
+    for partner in partners:
+        pl.semaphore_signal(barrier, inc=1, device_id=partner, device_id_type=MESH)
+    pl.semaphore_wait(barrier, len(partners))
+
+    def there(dx, dy):
+        ok = None
+        for d, here, count in ((dx, gx, nx), (dy, gy, ny)):
+            if d:
+                one = here > 0 if d < 0 else here < count - 1
+                ok = one if ok is None else ok & one
+        return ok
+
     copies = []
 
-    def launch(src, dst, where):
+    def launch(src, dst, step):
         index = len(copies)
         copy = pltpu.make_async_remote_copy(
             src_ref=src,
             dst_ref=dst,
             send_sem=send.at[index],
             recv_sem=recv.at[index],
-            device_id=where,
+            device_id=at(*step),
             device_id_type=MESH,
         )
-        copy.start()
-        copies.append(copy)
+        copies.append((copy, step))
+        pl.when(there(*step))(copy.start)
 
     for side in range(2):
-        step = 2 * side - 1
         near = pl.ds(0 if side == 0 else planes - HALO, HALO)
-        launch(bf.at[:, near], xb.at[1 - side], at(step, 0))
-        launch(fx.at[:, near], xf.at[1 - side], at(step, 0))
-        launch(ys.at[side], yh.at[1 - side], at(0, step))
+        launch(bf_far.at[:, near], xb.at[1 - side], (2 * side - 1, 0))
+        launch(fx_far.at[:, near], xf.at[1 - side], (2 * side - 1, 0))
+    for fetch in fetches:
+        fetch.wait()
+    for side in range(2):
+        begin_row = 0 if side == 0 else rows - HALO
+        for c in range(3):
+            span = slice(HALO * c, HALO * c + HALO)
+            ys[side, :, 0, span, :] = bf[c, :, begin_row : begin_row + HALO, :]
+            ys[side, :, 1, span, :] = 1.0 - fx[c, :, begin_row : begin_row + HALO, :].astype(f32)
+        ys[side, :, :, 3 * HALO :, :] = jnp.zeros((planes, 2, 8 - 3 * HALO, height), f32)
+    for side in range(2):
+        launch(ys.at[side], yh.at[1 - side], (0, 2 * side - 1))
+        near = pl.ds(0 if side == 0 else planes - HALO, HALO)
         for other in range(2):
             launch(
-                ys.at[other, near], ch.at[1 - side, 1 - other], at(step, 2 * other - 1)
+                ys.at[other, near], ch.at[1 - side, 1 - other], (2 * side - 1, 2 * other - 1)
             )
-    for copy in copies:
-        copy.wait()
-
-
-def sum_kernel(mine, total, along, across, part, send, recv):
-    gx, gy = lax.axis_index("gx"), lax.axis_index("gy")
-    nx, ny = lax.axis_size("gx"), lax.axis_size("gy")
-    barrier = pltpu.get_barrier_semaphore()
-    for k in range(1, nx):
-        pl.semaphore_signal(
-            barrier, inc=1, device_id=(lax.rem(gx + k, nx), gy), device_id_type=MESH
-        )
-    for k in range(1, ny):
-        pl.semaphore_signal(
-            barrier, inc=1, device_id=(gx, lax.rem(gy + k, ny)), device_id_type=MESH
-        )
-    pl.semaphore_wait(barrier, nx + ny - 2)
-
-    def exchange(src, dst, count, base, where):
-        copies = []
-        for k in range(1, count):
-            copy = pltpu.make_async_remote_copy(
-                src_ref=src,
-                dst_ref=dst.at[k - 1],
-                send_sem=send.at[base + k - 1],
-                recv_sem=recv.at[base + k - 1],
-                device_id=where(k),
-                device_id_type=MESH,
-            )
-            copy.start()
-            copies.append(copy)
-        for copy in copies:
-            copy.wait()
-
-    exchange(mine, along, nx, 0, lambda k: (lax.rem(gx + k, nx), gy))
-    part[...] = mine[...] + jnp.sum(along[...], axis=0)
-    exchange(part, across, ny, nx - 1, lambda k: (gx, lax.rem(gy + k, ny)))
-    total[...] = part[...] + jnp.sum(across[...], axis=0)
-
-
-def split(value):
-    high = value.astype(bf16)
-    return high, (value - high.astype(f32)).astype(bf16)
-
-
-def work_kernel(
-    bf, fx, xb, xf, yh, ch, nodes, loads, freq, hw, hb, ow, ob,
-    z_out, q_out, dens, sums,
-    wide, up, filt, ye, inv_s, force, free_s, z_s, q_s,
-):
-    gx, gy = lax.axis_index("gx"), lax.axis_index("gy")
-    nx, ny = lax.axis_size("gx"), lax.axis_size("gy")
-    planes, rows, height = bf.shape[1], bf.shape[2], bf.shape[3]
+
     cx, cy, cz = planes // CF + 2, rows // CF + 2, height // CF
     tall = cy * CF
     deep = planes + 2 * HALO
@@ -227,18 +208,8 @@
 
     lax.fori_loop(0, deep + 1, filtered, 0)
 
-    count = nodes.shape[0]
-    eye = (
-        lax.broadcasted_iota(jnp.int32, (8, 3), 0) == lax.broadcasted_iota(jnp.int32, (8, 3), 1)
-    ).astype(f32)
-    flat = lax.dot_general(
-        eye,
-        nodes[...].astype(f32),
-        (((1,), (1,)), ((), ())),
-        precision=lax.Precision.HIGHEST,
-        preferred_element_type=f32,
-    )
-    flat = (flat + 0.5).astype(jnp.int32)
+    count = nodes.shape[1]
+    flat = nodes[...]
     local_x = flat[0:1] - gx * planes + HALO
     local_y = flat[1:2] - gy * rows + CF
     near = (local_x >= 0) & (local_x < deep) & (local_y >= 0) & (local_y < tall)
@@ -266,6 +237,10 @@
         return 0
 
     lax.fori_loop(0, deep // group, place_loads, 0)
+
+    for copy, (dx, dy) in copies:
+        pl.when(there(dx, dy))(copy.wait_send)
+        pl.when(there(-dx, -dy))(copy.wait_recv)
 
     edge = CF - HALO
     for ref in (force, free_s):
@@ -406,11 +381,46 @@
         return (*highs, sum_d + fold(part * counted))
 
     *_, sum_d = lax.fori_loop(1, HALO + planes, second, (blank, blank, blank, zero))
-    z_out[...] = z_s[:, HALO : HALO + planes, own]
-    q_out[...] = q_s[:, HALO : HALO + planes, own]
-    sums[...] = jnp.zeros_like(sums)
+    mine[...] = jnp.zeros_like(mine)
     for index, value in enumerate((sum_a, sum_b, sum_c, sum_d)):
-        sums[index : index + 1, :] = jnp.sum(value, axis=0, keepdims=True)
+        mine[index : index + 1, :] = jnp.sum(value, axis=0, keepdims=True)
+
+    def exchange(src, dst, size, base, where):
+        moves = []
+        for k in range(1, size):
+            move = pltpu.make_async_remote_copy(
+                src_ref=src,
+                dst_ref=dst.at[k - 1],
+                send_sem=sum_send.at[base + k - 1],
+                recv_sem=sum_recv.at[base + k - 1],
+                device_id=where(k),
+                device_id_type=MESH,
+            )
+            move.start()
+            moves.append(move)
+        for move in moves:
+            move.wait()
+
+    exchange(mine, along, nx, 0, lambda k: at(k, 0))
+    part[...] = mine[...] + jnp.sum(along[...], axis=0)
+    exchange(part, across, ny, nx - 1, lambda k: at(0, k))
+    total = jnp.sum(part[...] + jnp.sum(across[...], axis=0), axis=1, keepdims=True)
+    a, b, c, d = (total[i : i + 1] for i in range(4))
+    alpha = a / b
+    next_rz = a - 2.0 * alpha * b + alpha * alpha * c
+    beta = next_rz / a
+    bent = b - 2.0 * alpha * c + alpha * alpha * d
+    energy = bent + 2.0 * beta * (b - alpha * c) + beta * beta * b
+    alpha_next = next_rz / energy
+    on_z = jnp.broadcast_to(alpha + alpha_next * (1.0 + beta), (rows, height))
+    on_q = jnp.broadcast_to(alpha_next * alpha, (rows, height))
+
+    def finish(i, _):
+        for k in range(3):
+            x_out[k, i] = on_z * z_s[k, i + HALO, own] - on_q * q_s[k, i + HALO, own]
+        return 0
+
+    lax.fori_loop(0, planes, finish, 0)
 
 
 def per_device(bf, fx, nodes, loads, freq, hw, hb, ow, ob):
@@ -420,36 +430,28 @@
     halo = (2, 3, HALO, rows, height)
     packed = (2, planes, 2, 8, height)
     corner = (2, 2, HALO, 2, 8, height)
-    xb, xf, yh, ch = pl.pallas_call(
-        halo_kernel,
-        out_shape=[
-            shape(halo, f32), shape(halo, jnp.int32), shape(packed, f32), shape(corner, f32)
-        ],
-        in_specs=[FULL] * 2,
-        out_specs=[FULL] * 4,
-        scratch_shapes=[
-            pltpu.VMEM(packed, f32),
-            pltpu.SemaphoreType.DMA((10,)),
-            pltpu.SemaphoreType.DMA((10,)),
-        ],
-        compiler_params=pltpu.CompilerParams(
-            collective_id=0, has_side_effects=True, vmem_limit_bytes=16 << 20
-        ),
-    )(bf, fx)
     cx, tall, deep = planes // CF + 2, rows + 2 * CF, planes + 2 * HALO
     width = hw.shape[2]
     field = pltpu.VMEM((3, deep, tall, height), f32)
-    z0, q, density, sums = pl.pallas_call(
-        work_kernel,
-        out_shape=[
-            shape(bf.shape, f32),
-            shape(bf.shape, f32),
-            shape(bf.shape[1:], f32),
-            shape((8, height), f32),
-        ],
-        in_specs=[FULL] * 12 + [pl.BlockSpec(memory_space=pltpu.SMEM)],
-        out_specs=[FULL] * 4,
+    far = pl.BlockSpec(memory_space=pl.ANY)
+    tile = (8, height)
+    return pl.pallas_call(
+        whole_kernel,
+        out_shape=[shape(bf.shape, f32), shape(bf.shape[1:], f32)],
+        in_specs=[far] * 2 + [FULL] * 6 + [pl.BlockSpec(memory_space=pltpu.SMEM)],
+        out_specs=[FULL] * 2,
         scratch_shapes=[
+            pltpu.VMEM(bf.shape, f32),
+            pltpu.VMEM(fx.shape, jnp.int32),
+            pltpu.VMEM(halo, f32),
+            pltpu.VMEM(halo, jnp.int32),
+            pltpu.VMEM(packed, f32),
+            pltpu.VMEM(corner, f32),
+            pltpu.VMEM(packed, f32),
+            pltpu.VMEM((nx - 1, *tile), f32),
+            pltpu.VMEM((ny - 1, *tile), f32),
+            pltpu.VMEM(tile, f32),
+            pltpu.VMEM(tile, f32),
             pltpu.VMEM((hw.shape[0], 2 * width, 2 * width), bf16),
             pltpu.VMEM((cx, tall, height), f32),
             pltpu.VMEM((4, cx, tall, height), f32),
@@ -459,36 +461,16 @@
             field,
             field,
             field,
-        ],
-        compiler_params=pltpu.CompilerParams(vmem_limit_bytes=40 << 20),
-    )(bf, fx, xb, xf, yh, ch, nodes, loads, freq, hw, hb, ow.reshape(1, -1), ob.reshape(1, 1))
-    total = pl.pallas_call(
-        sum_kernel,
-        out_shape=shape(sums.shape, f32),
-        in_specs=[FULL],
-        out_specs=FULL,
-        scratch_shapes=[
-            pltpu.VMEM((nx - 1, *sums.shape), f32),
-            pltpu.VMEM((ny - 1, *sums.shape), f32),
-            pltpu.VMEM(sums.shape, f32),
+            pltpu.SemaphoreType.DMA((6,)),
+            pltpu.SemaphoreType.DMA((10,)),
+            pltpu.SemaphoreType.DMA((10,)),
             pltpu.SemaphoreType.DMA((nx + ny - 2,)),
             pltpu.SemaphoreType.DMA((nx + ny - 2,)),
         ],
         compiler_params=pltpu.CompilerParams(
-            collective_id=1, has_side_effects=True, vmem_limit_bytes=16 << 20
+            collective_id=0, has_side_effects=True, vmem_limit_bytes=50 << 20
         ),
-    )(sums)
-    scalars = jnp.sum(total, axis=1)
-    a, b, c, d = (scalars[i] for i in range(4))
-    alpha = a / b
-    next_rz = a - 2.0 * alpha * b + alpha * alpha * c
-    beta = next_rz / a
-    bent = b - 2.0 * alpha * c + alpha * alpha * d
-    energy = bent + 2.0 * beta * (b - alpha * c) + beta * beta * b
-    alpha_next = next_rz / energy
-    along_z = alpha + alpha_next * (1.0 + beta)
-    displacement = along_z * z0 - (alpha_next * alpha) * q
-    return displacement, density
+    )(bf, fx, nodes.T, loads, freq, hw, hb, ow.reshape(1, -1), ob.reshape(1, 1))
 
 
 def solution(mesh):

time: 63.4 us -> 45.5 us (0.72)
  Pallas kernels: 48.4 us -> 37 us
  between operations: 9.07 us -> 1.32 us
  local copies, waits for them, and re-layouts: 4.43 us -> 6.85 us
  other arithmetic: 1.16 us -> 0 us
    pallas_call x3 -> x1, Pallas kernels: 48.4 us -> 37 us  [per_device(): pl.pallas_call(whole_kernel, out_shape=[shape(bf.shape, f32), shape(bf.sh...]
    unnamed x19 -> x18, local copies, waits for them, and re-layouts: 3.79 us -> 6.85 us
    sub x1 -> x0, other arithmetic: 1.05 us -> none  [per_device(): displacement = along_z * z0 - alpha_next * alpha * q]
    slice x1 -> x0, local copies, waits for them, and re-layouts: 0.64 us -> none  [per_device(): a, b, c, d = (scalars[i] for i in range(4))]
where the time goes in v2:
time: 45.5 us; the launch traced here: 45.2 us
  Pallas kernels  37 us (81%)
  local copies, waits for them, and re-layouts  6.85 us (15%)
  between operations  1.32 us (3%)
    pallas_call x1, Pallas kernels, per_device(): pl.pallas_call(whole_kernel, out_shape=[shape(bf.shape, f32), shape(bf.sh...  37 us
    unnamed x18, local copies, waits for them, and re-layouts  6.85 us

profile of v2, /device:TPU:0, one launch (start us, length us, event | category | flops | bytes accessed | tf_op | source)
XLA Modules:
  0.0 45.2 jit_solution(15813221617203392319)
XLA Ops:
  1.3 0.0 copy-start.6
  1.3 0.0 copy-start.5
  1.3 0.0 copy-start.7
  1.3 0.7 %copy-done.6 = f32[3,128]{1,0:T(4,128)S(1)} copy-done((f32[3,128]{1,0:T(4,128)S(1)}, f32[3,128]{1,0:T(4,128)}, u32[]{:S(2)}) %copy-start.6) | copy-done | bytes 1560
  2.0 0.0 copy-done.5
  2.0 0.0 copy-done.7
  2.0 0.0 copy-start
  2.0 1.1 %copy-done = f32[3,16,32,128]{3,2,1,0:T(8,128)S(1)} copy-done((f32[3,16,32,128]{3,2,1,0:T(8,128)S(1)}, f32[3,16,32,128]{3,2,1,0:T(8,128)}, u32[]{:S(2)}) %copy-start) | copy-done | bytes 786456
  3.1 0.0 copy-start.1
  3.1 1.1 %copy-done.1 = s32[3,16,32,128]{3,2,1,0:T(8,128)S(1)} copy-done((s32[3,16,32,128]{3,2,1,0:T(8,128)S(1)}, s32[3,16,32,128]{3,2,1,0:T(8,128)}, u32[]{:S(2)}) %copy-start.1) | copy-done | bytes 786456
  4.2 0.0 copy-start.2
  4.3 0.9 %copy-done.2 = f32[3,128,128]{2,1,0:T(8,128)S(1)} copy-done((f32[3,128,128]{2,1,0:T(8,128)S(1)}, f32[3,128,128]{2,1,0:T(8,128)}, u32[]{:S(2)}) %copy-start.2) | copy-done | bytes 196632
  5.2 0.0 copy-start.3
  5.2 0.7 %copy-done.3 = s32[512,3]{0,1:T(4,128)S(1)} copy-done((s32[512,3]{0,1:T(4,128)S(1)}, s32[512,3]{0,1:T(4,128)}, u32[]{:S(2)}) %copy-start.3) | copy-done | bytes 6168
  5.9 0.0 copy-start.4
  5.9 0.7 %copy-done.4 = f32[3,512]{1,0:T(4,128)S(1)} copy-done((f32[3,512]{1,0:T(4,128)S(1)}, f32[3,512]{1,0:T(4,128)}, u32[]{:S(2)}) %copy-start.4) | copy-done | bytes 6168
  6.6 37.0 %shard_map.104 = (f32[3,16,32,128]{3,2,1,0:T(8,128)S(1)}, f32[16,32,128]{2,1,0:T(8,128)S(1)}) custom-call(f32[3,16,32,128]{3,2,1,0:T(8,128)S(1)} %copy-done, s32[3,16,32,128]{3,2,1,0:T(8,128)S(1)} %copy-done.1, s32[3,512]{1,0:T(4,128)S(1)} %bitcast.4, f32[3,512]{1,0:T(4,128)S(1)} %copy-done.4, f32[3,64]{1,0:T(4,128)S(1)} %copy-done.5, ...), custom_call_target="tpu_custom_call" | custom-call | tf_op jit(solution)/shard_map/pallas_call | solution.py:438
  43.6 0.9 %copy.14 = f32[3,16,32,128]{3,2,1,0:T(8,128)} copy(f32[3,16,32,128]{3,2,1,0:T(8,128)S(1)} %get-tuple-element.4) | data formatting | bytes 1572864
  44.5 0.7 %copy.15 = f32[16,32,128]{2,1,0:T(8,128)} copy(f32[16,32,128]{2,1,0:T(8,128)S(1)} %get-tuple-element.5) | data formatting | bytes 524288
Async XLA Ops:
  1.3 0.7 %copy-start.6 = (f32[3,128]{1,0:T(4,128)S(1)}, f32[3,128]{1,0:T(4,128)}, u32[]{:S(2)}) copy-start(f32[3,128]{1,0:T(4,128)} %hb.1) | copy-start | bytes 4612
  1.3 0.7 %copy-start.5 = (f32[3,64]{1,0:T(4,128)S(1)}, f32[3,64]{1,0:T(4,128)}, u32[]{:S(2)}) copy-start(f32[3,64]{1,0:T(4,128)} %freq.1) | copy-start | bytes 2308
  1.3 0.7 %copy-start.7 = (f32[128]{0:T(128)S(1)}, f32[128]{0:T(128)}, u32[]{:S(2)}) copy-start(f32[128]{0:T(128)} %param.16) | copy-start | bytes 1540
  2.0 1.1 %copy-start = (f32[3,16,32,128]{3,2,1,0:T(8,128)S(1)}, f32[3,16,32,128]{3,2,1,0:T(8,128)}, u32[]{:S(2)}) copy-start(f32[3,16,32,128]{3,2,1,0:T(8,128)} %bf_far.1) | copy-start | bytes 2359300
  3.1 1.1 %copy-start.1 = (s32[3,16,32,128]{3,2,1,0:T(8,128)S(1)}, s32[3,16,32,128]{3,2,1,0:T(8,128)}, u32[]{:S(2)}) copy-start(s32[3,16,32,128]{3,2,1,0:T(8,128)} %fx_far.1) | copy-start | bytes 2359300
  4.2 0.9 %copy-start.2 = (f32[3,128,128]{2,1,0:T(8,128)S(1)}, f32[3,128,128]{2,1,0:T(8,128)}, u32[]{:S(2)}) copy-start(f32[3,128,128]{2,1,0:T(8,128)} %hw.1) | copy-start | bytes 589828
  5.2 0.7 %copy-start.3 = (s32[512,3]{0,1:T(4,128)S(1)}, s32[512,3]{0,1:T(4,128)}, u32[]{:S(2)}) copy-start(s32[512,3]{0,1:T(4,128)} %param.11) | copy-start | bytes 18436
  5.9 0.7 %copy-start.4 = (f32[3,512]{1,0:T(4,128)S(1)}, f32[3,512]{1,0:T(4,128)}, u32[]{:S(2)}) copy-start(f32[3,512]{1,0:T(4,128)} %loads.1) | copy-start | bytes 18436

commit v3 on v2

--- a/solution.py
+++ b/solution.py
@@ -27,35 +27,36 @@
 
 
 def whole_kernel(
-    bf_far, fx_far, nodes, loads, freq, hw, hb, ow, ob,
+    bf_far, fx_far, nodes_far, loads_far, freq_far, hw_far, hb_far, ow_far, ob,
     x_out, dens,
-    bf, fx, xb, xf, yh, ch, ys, along, across, mine, part,
+    nodes, loads, freq, hw, hb, ow, bf, fx, xb, xf, yh, ch, ys, along, across, mine, part,
     wide, up, filt, ye, inv_s, force, free_s, z_s, q_s,
-    local, send, recv, sum_send, sum_recv,
+    modes_s, held, ready, local, send, recv, sum_send, sum_recv,
 ):
     gx, gy = lax.axis_index("gx"), lax.axis_index("gy")
     nx, ny = lax.axis_size("gx"), lax.axis_size("gy")
     planes, rows, height = bf.shape[1], bf.shape[2], bf.shape[3]
 
+    def at(dx, dy):
+        return (lax.rem(gx + dx + nx, nx), lax.rem(gy + dy + ny, ny))
+
+    barrier = pltpu.get_barrier_semaphore()
+    partners = [at(dx, dy) for dx in (-1, 1) for dy in (-1, 1)]
+    partners += [at(k, 0) for k in range(1, nx)] + [at(0, k) for k in range(1, ny)]
+    for partner in partners:
+        pl.semaphore_signal(barrier, inc=1, device_id=partner, device_id_type=MESH)
     fetches = []
     for c in range(3):
         for far, near, index in ((bf_far, bf, c), (fx_far, fx, 3 + c)):
             fetch = pltpu.make_async_copy(far.at[c], near.at[c], local.at[index])
             fetch.start()
             fetches.append(fetch)
-    for ref in (xb, xf, yh, ch):
-        ref[...] = jnp.zeros_like(ref)
-
-    def at(dx, dy):
-        return (lax.rem(gx + dx + nx, nx), lax.rem(gy + dy + ny, ny))
-
-    barrier = pltpu.get_barrier_semaphore()
-    partners = [at(dx, dy) for dx in (-1, 1) for dy in (-1, 1)]
-    partners += [at(k, 0) for k in range(1, nx)] + [at(0, k) for k in range(1, ny)]
-    for partner in partners:
-        pl.semaphore_signal(barrier, inc=1, device_id=partner, device_id_type=MESH)
-    pl.semaphore_wait(barrier, len(partners))
-
+    smalls = []
+    few = (freq_far, hw_far, hb_far, ow_far, nodes_far, loads_far)
+    for index, (far, near) in enumerate(zip(few, (freq, hw, hb, ow, nodes, loads))):
+        fetch = pltpu.make_async_copy(far, near, local.at[6 + index])
+        fetch.start()
+        smalls.append(fetch)
     def there(dx, dy):
         ok = None
         for d, here, count in ((dx, gx, nx), (dy, gy, ny)):
@@ -65,6 +66,7 @@
         return ok
 
     copies = []
+    landings = []
 
     def launch(src, dst, step):
         index = len(copies)
@@ -77,8 +79,10 @@
             device_id_type=MESH,
         )
         copies.append((copy, step))
+        landings.append(dst)
         pl.when(there(*step))(copy.start)
 
+    pl.semaphore_wait(barrier, len(partners))
     for side in range(2):
         near = pl.ds(0 if side == 0 else planes - HALO, HALO)
         launch(bf_far.at[:, near], xb.at[1 - side], (2 * side - 1, 0))
@@ -100,6 +104,8 @@
                 ys.at[other, near], ch.at[1 - side, 1 - other], (2 * side - 1, 2 * other - 1)
             )
 
+    for fetch in smalls:
+        fetch.wait()
     cx, cy, cz = planes // CF + 2, rows // CF + 2, height // CF
     tall = cy * CF
     deep = planes + 2 * HALO
@@ -169,7 +175,7 @@
             lhs = jnp.concatenate(split(hidden), axis=1)
             out = jnp.dot(lhs, wide[layer], preferred_element_type=f32)
             mixed = out[:, :width] + out[:, width:] + hb[layer : layer + 1, :]
-            hidden = mixed / (1.0 + jnp.exp(jnp.minimum(-mixed, 80.0)))
+            hidden = mixed * pl.reciprocal(1.0 + jnp.exp(jnp.minimum(-mixed, 80.0)))
         lhs = jnp.concatenate(split(hidden), axis=1)
         out = lax.dot_general(
             lhs, wide_out, (((1,), (1,)), ((), ())), preferred_element_type=f32
@@ -238,9 +244,13 @@
 
     lax.fori_loop(0, deep // group, place_loads, 0)
 
-    for copy, (dx, dy) in copies:
+    def clear(ref):
+        ref[...] = jnp.zeros(ref.shape, ref.dtype)
+
+    for (copy, (dx, dy)), landing in zip(copies, landings):
         pl.when(there(dx, dy))(copy.wait_send)
         pl.when(there(-dx, -dy))(copy.wait_recv)
+        pl.when(jnp.logical_not(there(-dx, -dy)))(functools.partial(clear, landing))
 
     edge = CF - HALO
     for ref in (force, free_s):
@@ -292,21 +302,31 @@
     zero = jnp.zeros((8, height), f32)
     sum_a = lax.fori_loop(0, deep, begin, zero)
 
-    def element_forces(src, e):
+    kinds = ("SS", "SD", "DS", "DD")
+
+    def transform(src, m):
+        slot = lax.rem(m, 2)
+        for c in range(3):
+            v = src[c, m]
+            w = up_y(v)
+            for k, t in ((0, v + w), (2, w - v)):
+                u = up_z(t)
+                modes_s[slot, 4 * c + k] = t + u
+                modes_s[slot, 4 * c + k + 1] = u - t
+
+    def mode_forces(e, span):
+        below, above = lax.rem(e, 2), lax.rem(e + 1, 2)
         modes = []
         for c in range(3):
-            low, high = src[c, e], src[c, e + 1]
             by = {}
-            for name_x, v in (("S", low + high), ("D", high - low)):
-                w = up_y(v)
-                for name_y, t in (("S", v + w), ("D", w - v)):
-                    u = up_z(t)
-                    if name_x + name_y != "SS":
-                        by[name_x + name_y + "S"] = t + u
-                    by[name_x + name_y + "D"] = u - t
+            for k, kind in enumerate(kinds):
+                low, high = modes_s[below, 4 * c + k, span], modes_s[above, 4 * c + k, span]
+                if k:
+                    by["S" + kind] = low + high
+                by["D" + kind] = high - low
             modes.append(by)
         x, y, z = modes
-        y1 = ye[e + 1] * (1.0 / 16.0)
+        y1 = ye[e + 1, span] * (1.0 / 16.0)
         y3 = y1 * (1.0 / 3.0)
         out = ({}, {}, {})
         trace = LAM * (x["DSS"] + y["SDS"] + z["SSD"])
@@ -334,53 +354,63 @@
         y9 = y1 * ((LAM + 4.0 * MU) / 9.0)
         for c in range(3):
             out[c]["DDD"] = y9 * modes[c]["DDD"]
-        lows, highs = [], []
-        for c in range(3):
-            by_x = []
-            for name_x in "SD":
-                by_y = []
-                for name_y in "SD":
-                    d = out[c][name_x + name_y + "D"]
-                    if name_x + name_y == "SS":
-                        by_y.append(down_z(d) - d)
-                    else:
-                        s = out[c][name_x + name_y + "S"]
-                        by_y.append((s - d) + down_z(s + d))
-                s, d = by_y
-                by_x.append((s - d) + down_y(s + d))
-            s, d = by_x
-            lows.append(s - d)
-            highs.append(s + d)
-        return lows, highs
+        for c in range(3):
+            for k, kind in enumerate(kinds):
+                d = out[c]["D" + kind]
+                if k:
+                    t = out[c]["S" + kind]
+                    lower, upper = t - d, t + d
+                else:
+                    lower, upper = -d, d
+                ready[4 * c + k, span] = held[4 * c + k, span] + lower
+                held[4 * c + k, span] = upper
+
+    def node_forces(src, e):
+        transform(src, e + 1)
+        for r in range(tall // 8):
+            mode_forces(e, slice(8 * r, 8 * r + 8))
+        forces = []
+        for c in range(3):
+            by_y = []
+            for k in (0, 2):
+                t, d = ready[4 * c + k], ready[4 * c + k + 1]
+                by_y.append((t - d) + down_z(t + d))
+            t, d = by_y
+            forces.append((t - d) + down_y(t + d))
+        return forces
+
+    def start_forces(src, e):
+        transform(src, e)
+        held[...] = jnp.zeros_like(held)
 
     def first(e, carry):
-        c0, c1, c2, sum_b, sum_c = carry
-        lows, highs = element_forces(z_s, e)
+        sum_b, sum_c = carry
+        forces = node_forces(z_s, e)
         inv = inv_s[e]
         counted = own_row * own_plane(e)
         part_b = jnp.zeros(plane, f32)
         part_c = jnp.zeros(plane, f32)
-        for c, before in enumerate((c0, c1, c2)):
-            w = free_s[c, e] * (before + lows[c])
+        for c in range(3):
+            w = free_s[c, e] * forces[c]
             q = w * inv
             q_s[c, e] = q
             part_b = part_b + w * z_s[c, e]
             part_c = part_c + w * q
-        return (*highs, sum_b + fold(part_b * counted), sum_c + fold(part_c * counted))
-
-    blank = jnp.zeros(plane, f32)
-    *_, sum_b, sum_c = lax.fori_loop(0, deep - 1, first, (blank, blank, blank, zero, zero))
-
-    def second(e, carry):
-        c0, c1, c2, sum_d = carry
-        lows, highs = element_forces(q_s, e)
+        return sum_b + fold(part_b * counted), sum_c + fold(part_c * counted)
+
+    start_forces(z_s, 0)
+    sum_b, sum_c = lax.fori_loop(0, deep - 1, first, (zero, zero))
+
+    def second(e, sum_d):
+        forces = node_forces(q_s, e)
         counted = own_row * own_plane(e)
         part = jnp.zeros(plane, f32)
-        for c, before in enumerate((c0, c1, c2)):
-            part = part + free_s[c, e] * (before + lows[c]) * q_s[c, e]
-        return (*highs, sum_d + fold(part * counted))
-
-    *_, sum_d = lax.fori_loop(1, HALO + planes, second, (blank, blank, blank, zero))
+        for c in range(3):
+            part = part + free_s[c, e] * forces[c] * q_s[c, e]
+        return sum_d + fold(part * counted)
+
+    start_forces(q_s, 1)
+    sum_d = lax.fori_loop(1, HALO + planes, second, zero)
     mine[...] = jnp.zeros_like(mine)
     for index, value in enumerate((sum_a, sum_b, sum_c, sum_d)):
         mine[index : index + 1, :] = jnp.sum(value, axis=0, keepdims=True)
@@ -438,9 +468,15 @@
     return pl.pallas_call(
         whole_kernel,
         out_shape=[shape(bf.shape, f32), shape(bf.shape[1:], f32)],
-        in_specs=[far] * 2 + [FULL] * 6 + [pl.BlockSpec(memory_space=pltpu.SMEM)],
+        in_specs=[far] * 8 + [pl.BlockSpec(memory_space=pltpu.SMEM)],
         out_specs=[FULL] * 2,
         scratch_shapes=[
+            pltpu.VMEM((nodes.shape[1], nodes.shape[0]), jnp.int32),
+            pltpu.VMEM(loads.shape, f32),
+            pltpu.VMEM(freq.shape, f32),
+            pltpu.VMEM(hw.shape, f32),
+            pltpu.VMEM(hb.shape, f32),
+            pltpu.VMEM((1, width), f32),
             pltpu.VMEM(bf.shape, f32),
             pltpu.VMEM(fx.shape, jnp.int32),
             pltpu.VMEM(halo, f32),
@@ -461,14 +497,17 @@
             field,
             field,
             field,
-            pltpu.SemaphoreType.DMA((6,)),
+            pltpu.VMEM((2, 12, tall, height), f32),
+            pltpu.VMEM((12, tall, height), f32),
+            pltpu.VMEM((12, tall, height), f32),
+            pltpu.SemaphoreType.DMA((12,)),
             pltpu.SemaphoreType.DMA((10,)),
             pltpu.SemaphoreType.DMA((10,)),
             pltpu.SemaphoreType.DMA((nx + ny - 2,)),
             pltpu.SemaphoreType.DMA((nx + ny - 2,)),
         ],
         compiler_params=pltpu.CompilerParams(
-            collective_id=0, has_side_effects=True, vmem_limit_bytes=50 << 20
+            collective_id=0, has_side_effects=True, vmem_limit_bytes=64 << 20
         ),
     )(bf, fx, nodes.T, loads, freq, hw, hb, ow.reshape(1, -1), ob.reshape(1, 1))
 

time: 45.5 us -> 42 us (0.923)
  local copies, waits for them, and re-layouts: 6.85 us -> 2.81 us
  Pallas kernels: 37 us -> 37.7 us
    unnamed x18 -> x4, local copies, waits for them, and re-layouts: 6.85 us -> 2.81 us
    pallas_call x1, Pallas kernels: 37 us -> 37.7 us  [per_device(): pl.pallas_call(whole_kernel, out_shape=[shape(bf.shape, f32), shape(bf.sh...]
where the time goes in v3:
time: 42 us; the launch traced here: 41.8 us
  Pallas kernels  37.7 us (90%)
  local copies, waits for them, and re-layouts  2.81 us (7%)
  between operations  1.3 us (3%)
    pallas_call x1, Pallas kernels, per_device(): pl.pallas_call(whole_kernel, out_shape=[shape(bf.shape, f32), shape(bf.sh...  37.7 us
    unnamed x4, local copies, waits for them, and re-layouts  2.81 us

profile of v3, /device:TPU:0, one launch (start us, length us, event | category | flops | bytes accessed | tf_op | source)
XLA Modules:
  0.0 41.8 jit_solution(14942595765554146130)
XLA Ops:
  1.3 37.7 %shard_map.104 = (f32[3,16,32,128]{3,2,1,0:T(8,128)}, f32[16,32,128]{2,1,0:T(8,128)}) custom-call(f32[3,16,32,128]{3,2,1,0:T(8,128)} %bf_far.1, s32[3,16,32,128]{3,2,1,0:T(8,128)} %fx_far.1, s32[3,512]{1,0:T(4,128)} %bitcast.4, f32[3,512]{1,0:T(4,128)} %loads_far.1, f32[3,64]{1,0:T(4,128)} %freq_far.1, f32[3,128,128]{2,1,0:T(8,128)} %hw_far.1, ...), custom_call_target="tpu_custom_call" | custom-call | tf_op jit(solution)/shard_map/pallas_call | solution.py:468
  39.0 0.0 copy-start
  39.0 2.1 %copy.14 = f32[3,16,32,128]{3,2,1,0:T(8,128)} copy(f32[3,16,32,128]{3,2,1,0:T(8,128)} %get-tuple-element.4) | data formatting | bytes 1572864
  41.1 0.0 copy-done
  41.1 0.7 %copy.15 = f32[16,32,128]{2,1,0:T(8,128)} copy(f32[16,32,128]{2,1,0:T(8,128)S(1)} %copy-done) | data formatting | bytes 524288
Async XLA Ops:
  39.0 2.1 %copy-start = (f32[16,32,128]{2,1,0:T(8,128)S(1)}, f32[16,32,128]{2,1,0:T(8,128)}, u32[]{:S(2)}) copy-start(f32[16,32,128]{2,1,0:T(8,128)} %get-tuple-element.5) | copy-start | bytes 786436

commit v4 on v3

--- a/solution.py
+++ b/solution.py
@@ -31,7 +31,7 @@
     x_out, dens,
     nodes, loads, freq, hw, hb, ow, bf, fx, xb, xf, yh, ch, ys, along, across, mine, part,
     wide, up, filt, ye, inv_s, force, free_s, z_s, q_s,
-    modes_s, held, ready, local, send, recv, sum_send, sum_recv,
+    modes_s, held, ready, saved, local, send, recv, sum_send, sum_recv,
 ):
     gx, gy = lax.axis_index("gx"), lax.axis_index("gy")
     nx, ny = lax.axis_size("gx"), lax.axis_size("gy")
@@ -161,7 +161,7 @@
         lax.broadcasted_iota(jnp.int32, (cz, height), 1) // CF
         == lax.broadcasted_iota(jnp.int32, (cz, height), 0)
     ).astype(f32)
-    bias_out = ob[0, 0]
+    bias_out = ob[0]
 
     def cells(ix, _):
         index_x = gx * (planes // CF) - 1 + ix
@@ -247,10 +247,16 @@
     def clear(ref):
         ref[...] = jnp.zeros(ref.shape, ref.dtype)
 
-    for (copy, (dx, dy)), landing in zip(copies, landings):
-        pl.when(there(dx, dy))(copy.wait_send)
-        pl.when(there(-dx, -dy))(copy.wait_recv)
-        pl.when(jnp.logical_not(there(-dx, -dy)))(functools.partial(clear, landing))
+    def settle(chosen):
+        for index in chosen:
+            (copy, (dx, dy)), landing = copies[index], landings[index]
+            pl.when(there(dx, dy))(copy.wait_send)
+            pl.when(there(-dx, -dy))(copy.wait_recv)
+            pl.when(jnp.logical_not(there(-dx, -dy)))(functools.partial(clear, landing))
+
+    beside_y = [i for i, (_, step) in enumerate(copies) if step[0] == 0]
+    beside_x = [i for i, (_, step) in enumerate(copies) if step[0] != 0]
+    settle(beside_y)
 
     edge = CF - HALO
     for ref in (force, free_s):
@@ -259,20 +265,32 @@
     own = slice(CF, CF + rows)
     force[:, HALO : HALO + planes, own] = bf[...]
     free_s[:, HALO : HALO + planes, own] = 1.0 - fx[...].astype(f32)
+    def halo_rows(side):
+        start = edge if side == 0 else CF + rows
+        return slice(start, start + HALO)
+
+    def halo_planes(side):
+        start = 0 if side == 0 else deep - HALO
+        return slice(start, start + HALO)
+
     for side in range(2):
-        first = 0 if side == 0 else deep - HALO
-        force[:, first : first + HALO, own] = xb[side]
-        free_s[:, first : first + HALO, own] = 1.0 - xf[side].astype(f32)
-        start = edge if side == 0 else CF + rows
         for c in range(3):
             span = slice(HALO * c, HALO * c + HALO)
             for ref, which in ((force, 0), (free_s, 1)):
-                ref[c, HALO : HALO + planes, start : start + HALO] = yh[side, :, which, span]
-                for other in range(2):
-                    begin = 0 if other == 0 else deep - HALO
-                    ref[c, begin : begin + HALO, start : start + HALO] = ch[
-                        other, side, :, which, span
-                    ]
+                ref[c, HALO : HALO + planes, halo_rows(side)] = yh[side, :, which, span]
+
+    def place_x_halos():
+        for side in range(2):
+            force[:, halo_planes(side), own] = xb[side]
+            free_s[:, halo_planes(side), own] = 1.0 - xf[side].astype(f32)
+            for c in range(3):
+                span = slice(HALO * c, HALO * c + HALO)
+                for ref, which in ((force, 0), (free_s, 1)):
+                    for other in range(2):
+                        ref[c, halo_planes(other), halo_rows(side)] = ch[
+                            other, side, :, which, span
+                        ]
+
     node_row = gy * rows - CF + row
     in_y = ((node_row >= 0) & (node_row < ny * rows)).astype(f32)
 
@@ -300,7 +318,7 @@
         return total + fold(part * counted)
 
     zero = jnp.zeros((8, height), f32)
-    sum_a = lax.fori_loop(0, deep, begin, zero)
+    sum_a = lax.fori_loop(HALO, HALO + planes, begin, zero)
 
     kinds = ("SS", "SD", "DS", "DD")
 
@@ -365,10 +383,12 @@
                 ready[4 * c + k, span] = held[4 * c + k, span] + lower
                 held[4 * c + k, span] = upper
 
-    def node_forces(src, e):
+    def advance(src, e):
         transform(src, e + 1)
         for r in range(tall // 8):
             mode_forces(e, slice(8 * r, 8 * r + 8))
+
+    def gather():
         forces = []
         for c in range(3):
             by_y = []
@@ -383,9 +403,9 @@
         transform(src, e)
         held[...] = jnp.zeros_like(held)
 
-    def first(e, carry):
+    def first_node(e, carry):
         sum_b, sum_c = carry
-        forces = node_forces(z_s, e)
+        forces = gather()
         inv = inv_s[e]
         counted = own_row * own_plane(e)
         part_b = jnp.zeros(plane, f32)
@@ -398,11 +418,29 @@
             part_c = part_c + w * q
         return sum_b + fold(part_b * counted), sum_c + fold(part_c * counted)
 
+    def first(e, carry):
+        advance(z_s, e)
+        return first_node(e, carry)
+
+    start_forces(z_s, HALO)
+    advance(z_s, HALO)
+    saved[...] = ready[...]
+    last = HALO + planes - 1
+    carry = lax.fori_loop(HALO + 1, last, first, (zero, zero))
+    settle(beside_x)
+    place_x_halos()
+    lax.fori_loop(0, HALO, begin, zero)
+    lax.fori_loop(deep - HALO, deep, begin, zero)
+    carry = lax.fori_loop(last, last + 2, first, carry)
     start_forces(z_s, 0)
-    sum_b, sum_c = lax.fori_loop(0, deep - 1, first, (zero, zero))
+    advance(z_s, 0)
+    carry = lax.fori_loop(1, HALO, first, carry)
+    ready[...] = held[...] + saved[...]
+    sum_b, sum_c = first_node(HALO, carry)
 
     def second(e, sum_d):
-        forces = node_forces(q_s, e)
+        advance(q_s, e)
+        forces = gather()
         counted = own_row * own_plane(e)
         part = jnp.zeros(plane, f32)
         for c in range(3):
@@ -465,7 +503,7 @@
     field = pltpu.VMEM((3, deep, tall, height), f32)
     far = pl.BlockSpec(memory_space=pl.ANY)
     tile = (8, height)
-    return pl.pallas_call(
+    displacement, density = pl.pallas_call(
         whole_kernel,
         out_shape=[shape(bf.shape, f32), shape(bf.shape[1:], f32)],
         in_specs=[far] * 8 + [pl.BlockSpec(memory_space=pltpu.SMEM)],
@@ -500,6 +538,7 @@
             pltpu.VMEM((2, 12, tall, height), f32),
             pltpu.VMEM((12, tall, height), f32),
             pltpu.VMEM((12, tall, height), f32),
+            pltpu.VMEM((12, tall, height), f32),
             pltpu.SemaphoreType.DMA((12,)),
             pltpu.SemaphoreType.DMA((10,)),
             pltpu.SemaphoreType.DMA((10,)),
@@ -509,7 +548,8 @@
         compiler_params=pltpu.CompilerParams(
             collective_id=0, has_side_effects=True, vmem_limit_bytes=64 << 20
         ),
-    )(bf, fx, nodes.T, loads, freq, hw, hb, ow.reshape(1, -1), ob.reshape(1, 1))
+    )(bf, fx, nodes.T, loads, freq, hw, hb, ow.reshape(1, -1), ob)
+    return jnp.where(fx == 0, displacement, 0.0), density
 
 
 def solution(mesh):

time: 42 us -> 39.5 us (0.940)
  Pallas kernels: 37.7 us -> 34.9 us
  other arithmetic: 0 us -> 2.44 us
  local copies, waits for them, and re-layouts: 2.81 us -> 0.71 us
    pallas_call x1, Pallas kernels: 37.7 us -> 34.9 us  [per_device(): pl.pallas_call(whole_kernel, out_shape=[shape(bf.shape, f32), shape(bf.sh...]
    select_n x0 -> x1, other arithmetic: none -> 2.44 us  [per_device(): return (jnp.where(fx == 0, displacement, 0.0), density)]
    unnamed x4 -> x3, local copies, waits for them, and re-layouts: 2.81 us -> 0.71 us
where the time goes in v4:
time: 39.5 us; the launch traced here: 39.4 us
  Pallas kernels  34.9 us (88%)
  other arithmetic  2.44 us (6%)
  between operations  1.3 us (3%)
  local copies, waits for them, and re-layouts  0.71 us (2%)
    pallas_call x1, Pallas kernels, per_device(): pl.pallas_call(whole_kernel, out_shape=[shape(bf.shape, f32), shape(bf.sh...  34.9 us
    select_n x1, other arithmetic, per_device(): return (jnp.where(fx == 0, displacement, 0.0), density)  2.44 us

profile of v4, /device:TPU:0, one launch (start us, length us, event | category | flops | bytes accessed | tf_op | source)
XLA Modules:
  0.0 39.4 jit_solution(14851310146576955064)
XLA Ops:
  1.3 34.9 %shard_map.104 = (f32[3,16,32,128]{3,2,1,0:T(8,128)}, f32[16,32,128]{2,1,0:T(8,128)}) custom-call(f32[3,16,32,128]{3,2,1,0:T(8,128)} %bf_far.1, s32[3,16,32,128]{3,2,1,0:T(8,128)} %fx_far.1, s32[3,512]{1,0:T(4,128)} %bitcast.2, f32[3,512]{1,0:T(4,128)} %loads_far.1, f32[3,64]{1,0:T(4,128)} %freq_far.1, f32[3,128,128]{2,1,0:T(8,128)} %hw_far.1, ...), custom_call_target="tpu_custom_call" | custom-call | tf_op jit(solution)/shard_map/pallas_call | solution.py:506
  36.2 0.0 copy-start
  36.2 2.4 %compare_select_fusion = f32[3,16,32,128]{3,2,1,0:T(8,128)} fusion(f32[3,16,32,128]{3,2,1,0:T(8,128)} %get-tuple-element.4, s32[3,16,32,128]{3,2,1,0:T(8,128)} %fx_far.1), kind=kLoop, calls=%fused_computation | loop fusion | flops 393216 | bytes 2359296 | tf_op jit(solution)/shard_map/jit(_where)/select_n | solution.py:552
  38.7 0.0 copy-done
  38.7 0.7 %copy.13 = f32[16,32,128]{2,1,0:T(8,128)} copy(f32[16,32,128]{2,1,0:T(8,128)S(1)} %copy-done) | data formatting | bytes 524288
Async XLA Ops:
  36.2 2.5 %copy-start = (f32[16,32,128]{2,1,0:T(8,128)S(1)}, f32[16,32,128]{2,1,0:T(8,128)}, u32[]{:S(2)}) copy-start(f32[16,32,128]{2,1,0:T(8,128)} %get-tuple-element.9) | copy-start | bytes 786436

commit v5 on v4

--- a/solution.py
+++ b/solution.py
@@ -163,14 +163,17 @@
     ).astype(f32)
     bias_out = ob[0]
 
-    def cells(ix, _):
-        index_x = gx * (planes // CF) - 1 + ix
-        inside_x = jnp.where((index_x >= 0) & (index_x < total_cx), 1.0, 0.0).astype(f32)
-        at_x = (index_x.astype(f32) + 0.5) / float(total_cx)
-        sin_u, cos_u = wave(turn_y + (at_x * turn[0:1] + quarter))
-        hidden = jnp.concatenate(
-            [sin_u[j : j + 1] * cos_v + cos_u[j : j + 1] * sin_v for j in range(cy)], axis=0
-        )
+    at_once = max(k for k in (1, 2, 3) if cx % k == 0)
+
+    def cells(step, _):
+        blocks = []
+        for k in range(at_once):
+            index_x = gx * (planes // CF) - 1 + step * at_once + k
+            at_x = (index_x.astype(f32) + 0.5) / float(total_cx)
+            sin_u, cos_u = wave(turn_y + (at_x * turn[0:1] + quarter))
+            for j in range(cy):
+                blocks.append(sin_u[j : j + 1] * cos_v + cos_u[j : j + 1] * sin_v)
+        hidden = jnp.concatenate(blocks, axis=0)
         for layer in range(layers):
             lhs = jnp.concatenate(split(hidden), axis=1)
             out = jnp.dot(lhs, wide[layer], preferred_element_type=f32)
@@ -180,22 +183,28 @@
         out = lax.dot_general(
             lhs, wide_out, (((1,), (1,)), ((), ())), preferred_element_type=f32
         )
-        spread = (out[:, :height] + out[:, height:]).reshape(cy, cz, height)
-        logits = jnp.sum(spread * pick[None], axis=1) + bias_out
-        coarse = 1.0 / (1.0 + jnp.exp(jnp.minimum(-logits, 80.0)))
-        for j in range(cy):
-            up[ix, CF * j : CF * j + CF, :] = jnp.broadcast_to(coarse[j : j + 1], (CF, height))
-        inside = inside_y * inside_x
-        for base, values in ((0, up[ix] * inside), (2, inside)):
-            beside = up_z(values) + down_z(values)
-            w2, w3 = 2.0 - math.sqrt(2.0), 2.0 - math.sqrt(3.0)
-            one = values + w2 * beside
-            two = w2 * values + w3 * beside
-            filt[base, ix] = 2.0 * values + beside + up_y(one) + down_y(one)
-            filt[base + 1, ix] = one + up_y(two) + down_y(two)
+        spread = (out[:, :height] + out[:, height:]).reshape(at_once, cy, cz, height)
+        for k in range(at_once):
+            ix = step * at_once + k
+            index_x = gx * (planes // CF) - 1 + ix
+            inside_x = jnp.where((index_x >= 0) & (index_x < total_cx), 1.0, 0.0).astype(f32)
+            logits = jnp.sum(spread[k] * pick[None], axis=1) + bias_out
+            coarse = 1.0 / (1.0 + jnp.exp(jnp.minimum(-logits, 80.0)))
+            for j in range(cy):
+                up[ix, CF * j : CF * j + CF, :] = jnp.broadcast_to(
+                    coarse[j : j + 1], (CF, height)
+                )
+            inside = inside_y * inside_x
+            for base, values in ((0, up[ix] * inside), (2, inside)):
+                beside = up_z(values) + down_z(values)
+                w2, w3 = 2.0 - math.sqrt(2.0), 2.0 - math.sqrt(3.0)
+                one = values + w2 * beside
+                two = w2 * values + w3 * beside
+                filt[base, ix] = 2.0 * values + beside + up_y(one) + down_y(one)
+                filt[base + 1, ix] = one + up_y(two) + down_y(two)
         return 0
 
-    lax.fori_loop(0, cx, cells, 0)
+    lax.fori_loop(0, cx // at_once, cells, 0)
 
     def filtered(i, _):
         here, back, ahead = (i + 1) // CF, i // CF, (i + 2) // CF
@@ -212,7 +221,7 @@
 
         return 0
 
-    lax.fori_loop(0, deep + 1, filtered, 0)
+    lax.fori_loop(0, deep + 1, filtered, 0, unroll=3)
 
     count = nodes.shape[1]
     flat = nodes[...]
@@ -318,7 +327,7 @@
         return total + fold(part * counted)
 
     zero = jnp.zeros((8, height), f32)
-    sum_a = lax.fori_loop(HALO, HALO + planes, begin, zero)
+    sum_a = lax.fori_loop(HALO, HALO + planes, begin, zero, unroll=2)
 
     kinds = ("SS", "SD", "DS", "DD")
 
@@ -488,7 +497,7 @@
             x_out[k, i] = on_z * z_s[k, i + HALO, own] - on_q * q_s[k, i + HALO, own]
         return 0
 
-    lax.fori_loop(0, planes, finish, 0)
+    lax.fori_loop(0, planes, finish, 0, unroll=4)
 
 
 def per_device(bf, fx, nodes, loads, freq, hw, hb, ow, ob):
@@ -546,7 +555,7 @@
             pltpu.SemaphoreType.DMA((nx + ny - 2,)),
         ],
         compiler_params=pltpu.CompilerParams(
-            collective_id=0, has_side_effects=True, vmem_limit_bytes=64 << 20
+            collective_id=0, has_side_effects=True, vmem_limit_bytes=63 << 20
         ),
     )(bf, fx, nodes.T, loads, freq, hw, hb, ow.reshape(1, -1), ob)
     return jnp.where(fx == 0, displacement, 0.0), density

time: 39.5 us -> 36 us (0.911)
  Pallas kernels: 34.9 us -> 31.6 us
    pallas_call x1, Pallas kernels: 34.9 us -> 31.6 us  [per_device(): pl.pallas_call(whole_kernel, out_shape=[shape(bf.shape, f32), shape(bf.sh...]
where the time goes in v5:
time: 36 us; the launch traced here: 35.9 us
  Pallas kernels  31.6 us (88%)
  other arithmetic  2.2 us (6%)
  between operations  1.31 us (4%)
  local copies, waits for them, and re-layouts  0.71 us (2%)
    pallas_call x1, Pallas kernels, per_device(): pl.pallas_call(whole_kernel, out_shape=[shape(bf.shape, f32), shape(bf.sh...  31.6 us
    select_n x1, other arithmetic, per_device(): return (jnp.where(fx == 0, displacement, 0.0), density)  2.2 us

profile of v5, /device:TPU:0, one launch (start us, length us, event | category | flops | bytes accessed | tf_op | source)
XLA Modules:
  0.0 35.9 jit_solution(8090476587049898374)
XLA Ops:
  1.3 0.0 copy-start
  1.3 31.6 %shard_map.104 = (f32[3,16,32,128]{3,2,1,0:T(8,128)}, f32[16,32,128]{2,1,0:T(8,128)}) custom-call(f32[3,16,32,128]{3,2,1,0:T(8,128)} %bf_far.1, s32[3,16,32,128]{3,2,1,0:T(8,128)} %fx_far.1, s32[3,512]{1,0:T(4,128)} %bitcast.2, f32[3,512]{1,0:T(4,128)} %loads_far.1, f32[3,64]{1,0:T(4,128)} %freq_far.1, f32[3,128,128]{2,1,0:T(8,128)} %hw_far.1, ...), custom_call_target="tpu_custom_call" | custom-call | tf_op jit(solution)/shard_map/pallas_call | solution.py:515
  32.9 0.0 copy-done
  32.9 0.0 copy-start.1
  32.9 2.2 %compare_select_fusion = f32[3,16,32,128]{3,2,1,0:T(8,128)} fusion(f32[3,16,32,128]{3,2,1,0:T(8,128)} %get-tuple-element.4, s32[3,16,32,128]{3,2,1,0:T(8,128)S(1)} %copy-done), kind=kLoop, calls=%fused_computation | loop fusion | flops 393216 | bytes 2359296 | tf_op jit(solution)/shard_map/jit(_where)/select_n | solution.py:561
  35.2 0.0 copy-done.1
  35.2 0.7 %copy.13 = f32[16,32,128]{2,1,0:T(8,128)} copy(f32[16,32,128]{2,1,0:T(8,128)S(1)} %copy-done.1) | data formatting | bytes 524288
Async XLA Ops:
  1.3 31.7 %copy-start = (s32[3,16,32,128]{3,2,1,0:T(8,128)S(1)}, s32[3,16,32,128]{3,2,1,0:T(8,128)}, u32[]{:S(2)}) copy-start(s32[3,16,32,128]{3,2,1,0:T(8,128)} %fx_far.1) | copy-start | bytes 2359300
  32.9 2.2 %copy-start.1 = (f32[16,32,128]{2,1,0:T(8,128)S(1)}, f32[16,32,128]{2,1,0:T(8,128)}, u32[]{:S(2)}) copy-start(f32[16,32,128]{2,1,0:T(8,128)} %get-tuple-element.9) | copy-start | bytes 786436

commit v6 on v5

--- a/solution.py
+++ b/solution.py
@@ -331,8 +331,7 @@
 
     kinds = ("SS", "SD", "DS", "DD")
 
-    def transform(src, m):
-        slot = lax.rem(m, 2)
+    def transform(src, m, slot):
         for c in range(3):
             v = src[c, m]
             w = up_y(v)
@@ -341,8 +340,8 @@
                 modes_s[slot, 4 * c + k] = t + u
                 modes_s[slot, 4 * c + k + 1] = u - t
 
-    def mode_forces(e, span):
-        below, above = lax.rem(e, 2), lax.rem(e + 1, 2)
+    def mode_forces(e, span, below):
+        above = 1 - below
         modes = []
         for c in range(3):
             by = {}
@@ -392,10 +391,10 @@
                 ready[4 * c + k, span] = held[4 * c + k, span] + lower
                 held[4 * c + k, span] = upper
 
-    def advance(src, e):
-        transform(src, e + 1)
+    def advance(src, e, below):
+        transform(src, e + 1, 1 - below)
         for r in range(tall // 8):
-            mode_forces(e, slice(8 * r, 8 * r + 8))
+            mode_forces(e, slice(8 * r, 8 * r + 8), below)
 
     def gather():
         forces = []
@@ -409,7 +408,7 @@
         return forces
 
     def start_forces(src, e):
-        transform(src, e)
+        transform(src, e, e % 2)
         held[...] = jnp.zeros_like(held)
 
     def first_node(e, carry):
@@ -427,28 +426,38 @@
             part_c = part_c + w * q
         return sum_b + fold(part_b * counted), sum_c + fold(part_c * counted)
 
-    def first(e, carry):
-        advance(z_s, e)
+    def first(e, carry, below):
+        advance(z_s, e, below)
         return first_node(e, carry)
 
+    def in_pairs(body, start, stop, carry):
+        def pair(i, carry):
+            e = start + 2 * i
+            return body(e + 1, body(e, carry, start % 2), 1 - start % 2)
+
+        carry = lax.fori_loop(0, (stop - start) // 2, pair, carry)
+        if (stop - start) % 2:
+            carry = body(jnp.int32(stop - 1), carry, (stop - 1) % 2)
+        return carry
+
     start_forces(z_s, HALO)
-    advance(z_s, HALO)
+    advance(z_s, HALO, HALO % 2)
     saved[...] = ready[...]
     last = HALO + planes - 1
-    carry = lax.fori_loop(HALO + 1, last, first, (zero, zero))
+    carry = in_pairs(first, HALO + 1, last, (zero, zero))
     settle(beside_x)
     place_x_halos()
     lax.fori_loop(0, HALO, begin, zero)
     lax.fori_loop(deep - HALO, deep, begin, zero)
-    carry = lax.fori_loop(last, last + 2, first, carry)
+    carry = in_pairs(first, last, last + 2, carry)
     start_forces(z_s, 0)
-    advance(z_s, 0)
-    carry = lax.fori_loop(1, HALO, first, carry)
+    advance(z_s, 0, 0)
+    carry = in_pairs(first, 1, HALO, carry)
     ready[...] = held[...] + saved[...]
     sum_b, sum_c = first_node(HALO, carry)
 
-    def second(e, sum_d):
-        advance(q_s, e)
+    def second(e, sum_d, below):
+        advance(q_s, e, below)
         forces = gather()
         counted = own_row * own_plane(e)
         part = jnp.zeros(plane, f32)
@@ -457,7 +466,7 @@
         return sum_d + fold(part * counted)
 
     start_forces(q_s, 1)
-    sum_d = lax.fori_loop(1, HALO + planes, second, zero)
+    sum_d = in_pairs(second, 1, HALO + planes, zero)
     mine[...] = jnp.zeros_like(mine)
     for index, value in enumerate((sum_a, sum_b, sum_c, sum_d)):
         mine[index : index + 1, :] = jnp.sum(value, axis=0, keepdims=True)

time: 36 us -> 34 us (0.944)
  Pallas kernels: 31.6 us -> 29.6 us
    pallas_call x1, Pallas kernels: 31.6 us -> 29.6 us  [per_device(): pl.pallas_call(whole_kernel, out_shape=[shape(bf.shape, f32), shape(bf.sh...]
where the time goes in v6:
time: 34 us; the launch traced here: 33.9 us
  Pallas kernels  29.6 us (87%)
  other arithmetic  2.2 us (6%)
  between operations  1.31 us (4%)
  local copies, waits for them, and re-layouts  0.71 us (2%)
    pallas_call x1, Pallas kernels, per_device(): pl.pallas_call(whole_kernel, out_shape=[shape(bf.shape, f32), shape(bf.sh...  29.6 us
    select_n x1, other arithmetic, per_device(): return (jnp.where(fx == 0, displacement, 0.0), density)  2.2 us
    unnamed x5, local copies, waits for them, and re-layouts  0.71 us

profile of v6, /device:TPU:0, one launch (start us, length us, event | category | flops | bytes accessed | tf_op | source)
XLA Modules:
  0.0 33.9 jit_solution(1735811570562432798)
XLA Ops:
  1.3 0.0 copy-start
  1.3 29.6 %shard_map.104 = (f32[3,16,32,128]{3,2,1,0:T(8,128)}, f32[16,32,128]{2,1,0:T(8,128)}) custom-call(f32[3,16,32,128]{3,2,1,0:T(8,128)} %bf_far.1, s32[3,16,32,128]{3,2,1,0:T(8,128)} %fx_far.1, s32[3,512]{1,0:T(4,128)} %bitcast.2, f32[3,512]{1,0:T(4,128)} %loads_far.1, f32[3,64]{1,0:T(4,128)} %freq_far.1, f32[3,128,128]{2,1,0:T(8,128)} %hw_far.1, ...), custom_call_target="tpu_custom_call" | custom-call | tf_op jit(solution)/shard_map/pallas_call | solution.py:524
  30.9 0.0 copy-done
  30.9 0.0 copy-start.1
  30.9 2.2 %compare_select_fusion = f32[3,16,32,128]{3,2,1,0:T(8,128)} fusion(f32[3,16,32,128]{3,2,1,0:T(8,128)} %get-tuple-element.4, s32[3,16,32,128]{3,2,1,0:T(8,128)S(1)} %copy-done), kind=kLoop, calls=%fused_computation | loop fusion | flops 393216 | bytes 2359296 | tf_op jit(solution)/shard_map/jit(_where)/select_n | solution.py:570
  33.2 0.0 copy-done.1
  33.2 0.7 %copy.13 = f32[16,32,128]{2,1,0:T(8,128)} copy(f32[16,32,128]{2,1,0:T(8,128)S(1)} %copy-done.1) | data formatting | bytes 524288
Async XLA Ops:
  1.3 29.7 %copy-start = (s32[3,16,32,128]{3,2,1,0:T(8,128)S(1)}, s32[3,16,32,128]{3,2,1,0:T(8,128)}, u32[]{:S(2)}) copy-start(s32[3,16,32,128]{3,2,1,0:T(8,128)} %fx_far.1) | copy-start | bytes 2359300
  30.9 2.2 %copy-start.1 = (f32[16,32,128]{2,1,0:T(8,128)S(1)}, f32[16,32,128]{2,1,0:T(8,128)}, u32[]{:S(2)}) copy-start(f32[16,32,128]{2,1,0:T(8,128)} %get-tuple-element.9) | copy-start | bytes 786436
